TPU v7x, 512 devices: a whole 4x8x8 slice. The times are simulated.
512 devices in a mesh: tm: 4 (over y_lo, core), lat: 4 (over y_hi), lon: 32 (over z, x).
Axes of the slice: x: 4, y: 8 (y_hi: 4, y_lo: 2; y = y_hi * 2 + y_lo), z: 8, core: 2. Of those that a mesh axis runs over, the one named last changes fastest.
Arguments:
- state: bfloat16 [4, 4, 137, 32, 8192], P('tm', None, None, 'lat', 'lon'), may hold values from -6 to 6
- band_counts: int32 [4, 4], P('tm', 'lat'), may hold values from 2 to 6
- dep_blocks: int32 [4, 32, 64, 6], P('tm', 'lat', 'lon'), may hold values from 0 to 63, as said below
- lon_entry: int32 [4, 32, 8192], P('tm', 'lat', 'lon'), may hold values from 0 to 5
- lon_offset: int32 [4, 32, 8192], P('tm', 'lat', 'lon'), may hold values from 1 to 125
- lon_frac: float32 [4, 32, 8192], P('tm', 'lat', 'lon'), may hold values from 0 to 1
- lat_offset: int32 [4, 32, 8192], P('tm', 'lat', 'lon'), may hold values from -1 to 0
- lat_frac: float32 [4, 32, 8192], P('tm', 'lat', 'lon'), may hold values from 0 to 1
Outputs:
- misfit: bfloat16 [4, 4, 137, 32, 8192], P('tm', None, None, 'lat', 'lon')
Inputs may be any that keep to these rules, and one draw needn't show every extreme that they name: `dep_blocks`: the list of a destination block names each of the 6 blocks of its latitude row that lie from 3 blocks west of the first block of the destination's tile to 1 block east of the tile's last block (block numbers taken modulo 64) exactly once, in an order drawn for each block.
All inputs are finite; a program needn't handle non-finite values.
Results may differ from a plain program's by a relative error of at most 0.0046.
Values may be sent and summed in bfloat16 or wider, within the bound.
No kernel may reach another device: no remote copies, remote signals or barrier semaphores. Data moves between devices by JAX's collectives and lax.ppermute only.
A program may use at most 64 MiB of HBM per device.

v0:
```python
import functools

import jax
import jax.numpy as jnp
from jax import lax
from jax.experimental import pallas as pl
from jax.experimental.pallas import tpu as pltpu
from jax.sharding import PartitionSpec as P

BLK = 128
AXES = ("tm", "lat", "lon")
VMEM_LIMIT = 16 * 1024 * 1024
VMEM = pl.BlockSpec(memory_space=pltpu.VMEM)


def params():
    return pltpu.CompilerParams(vmem_limit_bytes=VMEM_LIMIT)


def cubic(s):
    return (
        -s * (s - 1.0) * (s - 2.0) / 6.0,
        (s + 1.0) * (s - 1.0) * (s - 2.0) / 2.0,
        -(s + 1.0) * s * (s - 2.0) / 2.0,
        (s + 1.0) * s * (s - 1.0) / 6.0,
    )


def move(value, dest, windows):
    bands, tiles = lax.axis_size("lat"), lax.axis_size("lon")
    pairs = []
    for t in windows:
        for b in range(bands):
            for j in range(tiles):
                to = dest(t, b, j)
                if to is not None:
                    source = (t * bands + b) * tiles + j
                    pairs.append((source, (to[0] * bands + to[1]) * tiles + to[2]))
    return lax.ppermute(value, AXES, pairs)


def split_kernel(x_ref, whole_ref, west_ref, east_ref, *wide):
    depth, rows, cols = x_ref.shape
    padded = whole_ref.shape[1]
    for g, (half_ref, buf) in enumerate(zip((west_ref, east_ref), wide)):
        lanes = slice(g * BLK, (g + 1) * BLK)
        buf[: depth * rows] = x_ref[:, :, lanes].astype(jnp.float32).reshape(depth * rows, BLK)
        if padded > depth:
            buf[depth * rows :] = jnp.zeros(((padded - depth) * rows, BLK), jnp.float32)
        for r in range(rows):
            slab = buf[pl.ds(r, padded, stride=rows), :].astype(jnp.bfloat16)
            whole_ref[r, :, lanes] = slab
            half_ref[r] = slab


def split_rows(x):
    _, rows, cols = x.shape
    depth = -(-x.shape[0] // 16) * 16
    bf16 = jnp.bfloat16
    return pl.pallas_call(
        split_kernel,
        out_shape=(
            jax.ShapeDtypeStruct((rows, depth, cols), bf16),
            jax.ShapeDtypeStruct((rows, depth, cols // 2), bf16),
            jax.ShapeDtypeStruct((rows, depth, cols // 2), bf16),
        ),
        in_specs=[VMEM],
        out_specs=(VMEM, VMEM, VMEM),
        scratch_shapes=[pltpu.VMEM((depth * rows, BLK), jnp.float32)] * 2,
        compiler_params=params(),
        cost_estimate=pl.CostEstimate(flops=0, bytes_accessed=6 * x.size, transcendentals=0),
        name="split_rows",
    )(x)


def matrix_kernel(geo_ref, m_ref):
    r = pl.program_id(0)
    _, span, cols = m_ref.shape
    first = geo_ref[0, pl.ds(r, 1), :].astype(jnp.int32)
    weights = [w.astype(jnp.bfloat16).astype(jnp.float32) for w in cubic(geo_ref[1, pl.ds(r, 1), :])]
    step = BLK // 2
    for s in range(0, span, step):
        gap = lax.broadcasted_iota(jnp.int32, (step, cols), 0) - (first - s)
        value = jnp.where(gap == 0, weights[0], 0.0)
        for node in range(1, 4):
            value = jnp.where(gap == node, weights[node], value)
        m_ref[0, s : s + step, :] = value.astype(jnp.bfloat16)


def matrices(geo, span):
    _, rows, cols = geo.shape
    return pl.pallas_call(
        matrix_kernel,
        grid=(rows,),
        out_shape=jax.ShapeDtypeStruct((rows, span, cols), jnp.bfloat16),
        in_specs=[pl.BlockSpec(geo.shape, lambda r: (0, 0, 0))],
        out_specs=pl.BlockSpec((1, span, cols), lambda r: (r, 0, 0)),
        compiler_params=params(),
        cost_estimate=pl.CostEstimate(
            flops=9 * rows * span * cols, bytes_accessed=2 * rows * span * cols, transcendentals=0
        ),
        name="matrices",
    )(geo)


def row_product(far, near, west, own, m):
    outer = jnp.concatenate([far, near], axis=1)
    k = outer.shape[1]
    f32 = jnp.float32
    total = jnp.dot(outer, m[:k], preferred_element_type=f32)
    total += jnp.dot(west, m[k : 2 * k], preferred_element_type=f32)
    total += jnp.dot(own, m[2 * k :], preferred_element_type=f32)
    return total.astype(jnp.bfloat16)


def lon_kernel(*refs, per_step):
    ins, outs = refs[: 5 * per_step], refs[len(refs) - per_step :]
    for k in range(per_step):
        far, near, west, own, m = ins[5 * k : 5 * k + 5]
        outs[k][0] = row_product(far[0], near[0], west[0], own[0], m[0])


def lon_rows(far, near, west, own, m, firsts, count, after=()):
    _, depth, cols = own.shape
    arrays = (far, near, west, own, m)

    def at(array, first):
        return pl.BlockSpec((1,) + array.shape[1:], lambda i, first=first: (i + first, 0, 0))

    return pl.pallas_call(
        functools.partial(lon_kernel, per_step=len(firsts)),
        grid=(count,),
        out_shape=[jax.ShapeDtypeStruct((count, depth, cols), jnp.bfloat16) for _ in firsts],
        in_specs=[at(array, first) for first in firsts for array in arrays]
        + [pl.BlockSpec(memory_space=pl.ANY)] * len(after),
        out_specs=[pl.BlockSpec((1, depth, cols), lambda i: (i, 0, 0)) for _ in firsts],
        compiler_params=params(),
        cost_estimate=pl.CostEstimate(
            flops=2 * len(firsts) * count * depth * m.shape[1] * cols,
            bytes_accessed=2 * len(firsts) * count * (4 * depth * cols + m.shape[1] * cols),
            transcendentals=0,
        ),
        name="lon_rows",
    )(*(arrays * len(firsts)), *after)


def lat_kernel(above, top, mid, bot, below, geo_ref, out_ref, *wide):
    depth, rows, cols = out_ref.shape
    chunk = 48
    shift, weights = geo_ref[2].astype(jnp.int32), cubic(geo_ref[3])
    coefficients = []
    for distance in range(-2, 3):
        total = jnp.zeros_like(weights[0])
        for node in range(4):
            total += jnp.where(shift + node - 1 == distance, weights[node], 0.0)
        coefficients.append(total)
    padded = [(ref, i) for ref in (above, top, mid, bot, below) for i in range(ref.shape[0])]
    for low in range(0, depth, chunk):
        size = min(chunk, depth - low)
        for r in range(rows):
            total = None
            for k in range(5):
                ref, i = padded[r + k]
                term = coefficients[k][r : r + 1] * ref[i, low : low + size, :].astype(jnp.float32)
                total = term if total is None else total + term
            for g, buf in enumerate(wide):
                buf[pl.ds(low * rows + r, size, stride=rows), :] = total[:, g * BLK : (g + 1) * BLK]
        for g, buf in enumerate(wide):
            block = buf[low * rows : (low + size) * rows, :].astype(jnp.bfloat16)
            out_ref[low : low + size, :, g * BLK : (g + 1) * BLK] = block.reshape(size, rows, BLK)


def lat_rows(above, top, mid, bot, below, geo, depth):
    cols = mid.shape[2]
    rows = geo.shape[1]
    return pl.pallas_call(
        lat_kernel,
        out_shape=jax.ShapeDtypeStruct((depth, rows, cols), jnp.bfloat16),
        in_specs=[VMEM] * 6,
        out_specs=VMEM,
        scratch_shapes=[pltpu.VMEM((depth * rows, BLK), jnp.float32)] * (cols // BLK),
        compiler_params=params(),
        cost_estimate=pl.CostEstimate(
            flops=10 * depth * rows * cols, bytes_accessed=5 * depth * rows * cols, transcendentals=0
        ),
        name="lat_rows",
    )(above, top, mid, bot, below, geo)


def geometry(band_counts, dep_blocks, lon_entry, lon_offset, lon_frac, lat_offset, lat_frac):
    blocks, kmax = dep_blocks.shape[2:]
    cycle = blocks * lax.axis_size("lon")
    count, entry = band_counts[0, 0], lon_entry[0]
    slot = entry % count
    place = (dep_blocks[0] - lax.axis_index("lon") * blocks + blocks + blocks // 2) % cycle
    place = jnp.where(place == 0, 0, jnp.where(place == 3 * blocks - 1, 1, place + 1))
    place = jnp.repeat(place, BLK, axis=1)
    chosen = place[:, :, 0]
    for k in range(1, kmax):
        chosen = jnp.where(slot == k, place[:, :, k], chosen)
    first = chosen * BLK + lon_offset[0] - 1
    return jnp.stack(
        [first.astype(jnp.float32), lon_frac[0], lat_offset[0].astype(jnp.float32), lat_frac[0]]
    )


def body(state, *rest):
    fields_n, levels, rows, cols = state.shape[1:]
    depth = fields_n * levels
    windows, bands, tiles = (lax.axis_size(a) for a in AXES)
    flat = state.reshape(depth, rows, cols)
    cut = depth // 32 * 16
    tm = lax.axis_index("tm")

    def lend(t, b, j):
        return (3, b, j)

    geo_own = geometry(*rest)
    geo = jnp.where(tm == 3, move(geo_own, lend, (1,)), geo_own)
    second = jnp.where(tm == 3, move(flat[cut:], lend, (1,)), flat[cut:])
    m = matrices(geo, 3 * cols)

    ends, after = [], ()
    parts = (
        (flat[:cut], (0, 1, 2), {0: 1, 1: 2, 2: 3}),
        (second, (0, 2, 3), {0: 1, 3: 2, 2: 3}),
    )
    for part, active, onward in parts:
        own, west_half, east_half = split_rows(part)
        west = move(own, lambda t, b, j: (t, b, (j + 1) % tiles), active)
        near = move(west_half, lambda t, b, j: (t, b, (j - 1) % tiles), active)
        far = move(east_half, lambda t, b, j: (t, b, (j + 2) % tiles), active)
        top, bot = lon_rows(far, near, west, own, m, (0, rows - 2), 2, after)
        above = move(bot, lambda t, b, j: (t, b + 1, j) if b + 1 < bands else None, active)
        below = move(top, lambda t, b, j: (t, b - 1, j) if b > 0 else None, active)
        (mid,) = lon_rows(far, near, west, own, m, (2,), rows - 4)
        after = (mid,)
        end = lat_rows(above, top, mid, bot, below, geo, part.shape[0])
        ends.append(move(end, lambda t, b, j: (onward[t], b, j), active))
    previous = jnp.concatenate(ends, axis=0)
    misfit = (flat.astype(jnp.float32) - previous.astype(jnp.float32)).astype(jnp.bfloat16)
    return misfit.reshape(state.shape)


def solution(mesh):
    placed = (
        P("tm", None, None, "lat", "lon"),
        P("tm", "lat"),
        P("tm", "lat", "lon", None),
        P("tm", "lat", "lon"),
        P("tm", "lat", "lon"),
        P("tm", "lat", "lon"),
        P("tm", "lat", "lon"),
        P("tm", "lat", "lon"),
    )
    return jax.shard_map(
        body,
        mesh=mesh,
        in_specs=placed,
        out_specs=P("tm", None, None, "lat", "lon"),
        check_vma=False,
    )
```

profile of v0, /device:TPU:26, one launch (start us, length us, event | category | flops | bytes accessed | tf_op | source)
XLA Modules:
  0.0 137.9 jit_solution(8875010753107755997)
XLA Ops:
  0.0 2.3 %slice.40 = bf16[276,8,256]{2,1,0:T(8,128)(2,1)} slice(bf16[548,8,256]{2,1,0:T(8,128)(2,1)} %bitcast.52), slice={[272:548], [0:8], [0:256]} | slice | bytes 2260992 | tf_op jit(solution)/shard_map/slice | solution.py:220
  2.3 1.8 %collective-permute-start.7 = (bf16[276,8,256]{2,1,0:T(8,128)(2,1)}, bf16[276,8,256]{2,1,0:T(8,128)(2,1)}, u32[]{:S(2)}, u32[]{:S(2)}) collective-permute-start(bf16[276,8,256]{2,1,0:T(8,128)(2,1)} %slice.40), channel_id=1, source_target_pairs={{128,384},{129,385},{130,386},{131,387},{132,388},{133,389},{134,3... | collective-permute-start | bytes 3391496 | tf_op jit(solution)/shard_map/ppermute | solution.py:39
  4.1 1.3 slice.33.x_ref
  5.5 1.4 %split_rows.2 = (bf16[8,272,256]{2,1,0:T(8,128)(2,1)S(1)}, bf16[8,272,128]{2,1,0:T(8,128)(2,1)S(1)}, bf16[8,272,128]{2,1,0:T(8,128)(2,1)}) custom-call(bf16[272,8,256]{2,1,0:T(8,128)(2,1)S(1)} %slice.33.x_ref), custom_call_target="tpu_custom_call" | custom-call | bytes 3342336 | tf_op jit(solution)/shard_map/split_rows/pallas_call | solution.py:60
  6.9 3.4 %collective-permute-start.2 = (bf16[8,272,256]{2,1,0:T(8,128)(2,1)S(1)}, bf16[8,272,256]{2,1,0:T(8,128)(2,1)S(1)}, u32[]{:S(2)}, u32[]{:S(2)}) collective-permute-start(bf16[8,272,256]{2,1,0:T(8,128)(2,1)S(1)} %get-tuple-element.17.refs_3_.refs_8_), channel_id=1, source_target_pairs={{0,1},{1,2},{2,3},{3,4},{4,5},{5,6},{6,7},{7,8},{8,9},{9,10},{10,1... | collective-permute-start | bytes 3342344 | tf_op jit(solution)/shard_map/ppermute | solution.py:39
  10.3 4.8 %collective-permute-start = (bf16[8,272,128]{2,1,0:T(8,128)(2,1)}, bf16[8,272,128]{2,1,0:T(8,128)(2,1)S(1)}, u32[]{:S(2)}, u32[]{:S(2)}) collective-permute-start(bf16[8,272,128]{2,1,0:T(8,128)(2,1)} %get-tuple-element.15), channel_id=1, source_target_pairs={{0,2},{1,3},{2,4},{3,5},{4,6},{5,7},{6,8},{7,9},{8,10},{9,11},{10,... | collective-permute-start | bytes 1671176 | tf_op jit(solution)/shard_map/ppermute | solution.py:39
  15.9 1.4 %broadcast_select_fusion.x_ref = bf16[276,8,256]{2,1,0:T(8,128)(2,1)S(1)} fusion(bf16[276,8,256]{2,1,0:T(8,128)(2,1)} %collective-permute-done.7, pred[]{:T(512)S(6)} %eq.52, bf16[548,8,256]{2,1,0:T(8,128)(2,1)} %bitcast.54), kind=kLoop, calls=%fused_computation.3 | loop fusion | flops 565248 | bytes 3391489 | tf_op jit(solution)/shard_map/jit(_where)/select_n | solution.py:220
  17.3 0.6 split_rows.3
  17.9 2.8 %collective-permute-start.10 = (bf16[8,288,256]{2,1,0:T(8,128)(2,1)S(1)}, bf16[8,288,256]{2,1,0:T(8,128)(2,1)S(1)}, u32[]{:S(2)}, u32[]{:S(2)}) collective-permute-start(bf16[8,288,256]{2,1,0:T(8,128)(2,1)S(1)} %get-tuple-element.22.refs_3_.refs_8_), channel_id=1, source_target_pairs={{0,1},{1,2},{2,3},{3,4},{4,5},{5,6},{6,7},{7,8},{8,9},{9,10},{10,1... | collective-permute-start | bytes 3538952 | tf_op jit(solution)/shard_map/ppermute | solution.py:39
  21.0 0.7 collective-permute-start.3
  21.7 3.0 %collective-permute-start.1 = (bf16[8,272,128]{2,1,0:T(8,128)(2,1)S(1)}, bf16[8,272,128]{2,1,0:T(8,128)(2,1)S(1)}, u32[]{:S(2)}, u32[]{:S(2)}) collective-permute-start(bf16[8,272,128]{2,1,0:T(8,128)(2,1)S(1)} %get-tuple-element.16), channel_id=1, source_target_pairs={{0,31},{1,0},{2,1},{3,2},{4,3},{5,4},{6,5},{7,6},{8,7},{9,8},{10,9... | collective-permute-start | bytes 1671176 | tf_op jit(solution)/shard_map/ppermute | solution.py:39
  24.7 4.3 %collective-permute-start.8 = (bf16[8,288,128]{2,1,0:T(8,128)(2,1)S(1)}, bf16[8,288,128]{2,1,0:T(8,128)(2,1)S(1)}, u32[]{:S(2)}, u32[]{:S(2)}) collective-permute-start(bf16[8,288,128]{2,1,0:T(8,128)(2,1)S(1)} %get-tuple-element.20), channel_id=1, source_target_pairs={{0,2},{1,3},{2,4},{3,5},{4,6},{5,7},{6,8},{7,9},{8,10},{9,11},{10,... | collective-permute-start | bytes 1769480 | tf_op jit(solution)/shard_map/ppermute | solution.py:39
  29.1 23.7 %collective-permute-done.refs_0_.refs_5_ = bf16[8,272,128]{2,1,0:T(8,128)(2,1)S(1)} collective-permute-done((bf16[8,272,128]{2,1,0:T(8,128)(2,1)}, bf16[8,272,128]{2,1,0:T(8,128)(2,1)S(1)}, u32[]{:S(2)}, u32[]{:S(2)}) %collective-permute-start) | collective-permute-done | bytes 557088 | tf_op jit(solution)/shard_map/ppermute | solution.py:39
  52.8 1.9 %collective-permute-start.9 = (bf16[8,288,128]{2,1,0:T(8,128)(2,1)S(1)}, bf16[8,288,128]{2,1,0:T(8,128)(2,1)S(1)}, u32[]{:S(2)}, u32[]{:S(2)}) collective-permute-start(bf16[8,288,128]{2,1,0:T(8,128)(2,1)S(1)} %get-tuple-element.21), channel_id=1, source_target_pairs={{0,31},{1,0},{2,1},{3,2},{4,3},{5,4},{6,5},{7,6},{8,7},{9,8},{10,9... | collective-permute-start | bytes 1769480 | tf_op jit(solution)/shard_map/ppermute | solution.py:39
  54.7 2.1 %matrices.1.refs_4_.refs_9_ = bf16[8,768,256]{2,1,0:T(8,128)(2,1)S(1)} custom-call(f32[4,8,256]{2,1,0:T(8,128)S(1)} %broadcast_select_fusion.1.geo_ref), custom_call_target="tpu_custom_call" | custom-call | flops 14155776 | bytes 3145728 | tf_op jit(solution)/shard_map/matrices/pallas_call | solution.py:92
  56.9 1.2 lon_rows.5.mid.refs_10_
  58.1 31.3 %collective-permute-done.8.refs_0_.refs_5_ = bf16[8,288,128]{2,1,0:T(8,128)(2,1)S(1)} collective-permute-done((bf16[8,288,128]{2,1,0:T(8,128)(2,1)S(1)}, bf16[8,288,128]{2,1,0:T(8,128)(2,1)S(1)}, u32[]{:S(2)}, u32[]{:S(2)}) %collective-permute-start.8) | collective-permute-done | bytes 589856 | tf_op jit(solution)/shard_map/ppermute | solution.py:39
  89.3 0.8 lon_rows.6
  90.2 4.8 %collective-permute-start.11 = (bf16[2,288,256]{2,1,0:T(8,128)(2,1)S(1)}, bf16[2,288,256]{2,1,0:T(8,128)(2,1)S(1)}, u32[]{:S(2)}, u32[]{:S(2)}) collective-permute-start(bf16[2,288,256]{2,1,0:T(8,128)(2,1)S(1)} %get-tuple-element.23.bot), channel_id=1, source_target_pairs={{0,32},{1,33},{2,34},{3,35},{4,36},{5,37},{6,38},{7,39},{8,40},{9,... | collective-permute-start | bytes 884744 | tf_op jit(solution)/shard_map/ppermute | solution.py:39
  95.0 1.9 %collective-permute-start.12 = (bf16[2,288,256]{2,1,0:T(8,128)(2,1)S(1)}, bf16[2,288,256]{2,1,0:T(8,128)(2,1)S(1)}, u32[]{:S(2)}, u32[]{:S(2)}) collective-permute-start(bf16[2,288,256]{2,1,0:T(8,128)(2,1)S(1)} %get-tuple-element.24.top), channel_id=1, source_target_pairs={{32,0},{33,1},{34,2},{35,3},{36,4},{37,5},{38,6},{39,7},{40,8},{41... | collective-permute-start | bytes 884744 | tf_op jit(solution)/shard_map/ppermute | solution.py:39
  96.9 0.8 lon_rows.4
  97.8 6.0 %collective-permute-start.4 = (bf16[2,272,256]{2,1,0:T(8,128)(2,1)S(1)}, bf16[2,272,256]{2,1,0:T(8,128)(2,1)S(1)}, u32[]{:S(2)}, u32[]{:S(2)}) collective-permute-start(bf16[2,272,256]{2,1,0:T(8,128)(2,1)S(1)} %get-tuple-element.18.bot), channel_id=1, source_target_pairs={{0,32},{1,33},{2,34},{3,35},{4,36},{5,37},{6,38},{7,39},{8,40},{9,... | collective-permute-start | bytes 835592 | tf_op jit(solution)/shard_map/ppermute | solution.py:39
  103.8 1.9 %collective-permute-start.5 = (bf16[2,272,256]{2,1,0:T(8,128)(2,1)S(1)}, bf16[2,272,256]{2,1,0:T(8,128)(2,1)S(1)}, u32[]{:S(2)}, u32[]{:S(2)}) collective-permute-start(bf16[2,272,256]{2,1,0:T(8,128)(2,1)S(1)} %get-tuple-element.19.top), channel_id=1, source_target_pairs={{32,0},{33,1},{34,2},{35,3},{36,4},{37,5},{38,6},{39,7},{40,8},{41... | collective-permute-start | bytes 835592 | tf_op jit(solution)/shard_map/ppermute | solution.py:39
  105.7 1.2 lon_rows.7.mid
  106.9 2.0 %collective-permute-done.12.below = bf16[2,288,256]{2,1,0:T(8,128)(2,1)S(1)} collective-permute-done((bf16[2,288,256]{2,1,0:T(8,128)(2,1)S(1)}, bf16[2,288,256]{2,1,0:T(8,128)(2,1)S(1)}, u32[]{:S(2)}, u32[]{:S(2)}) %collective-permute-start.12) | collective-permute-done | bytes 294944 | tf_op jit(solution)/shard_map/ppermute | solution.py:39
  109.0 1.4 %lat_rows.3 = bf16[276,8,256]{2,1,0:T(8,128)(2,1)S(1)} custom-call(bf16[2,288,256]{2,1,0:T(8,128)(2,1)S(1)} %collective-permute-done.11.above, bf16[2,288,256]{2,1,0:T(8,128)(2,1)S(1)} %get-tuple-element.24.top, bf16[4,288,256]{2,1,0:T(8,128)(2,1)S(1)} %lon_rows.7.mid, bf16[2,288,256]{2,1,0:T(8,128)(2,1)S(1)} %get-tuple-element.23.bot, ...), custom_call_target="tpu_custom_call" | custom-call | flops 5652480 | bytes 2826240 | tf_op jit(solution)/shard_map/lat_rows/pallas_call | solution.py:176
  110.4 1.9 %collective-permute-start.13 = (bf16[276,8,256]{2,1,0:T(8,128)(2,1)S(1)}, bf16[276,8,256]{2,1,0:T(8,128)(2,1)S(1)}, u32[]{:S(2)}, u32[]{:S(2)}) collective-permute-start(bf16[276,8,256]{2,1,0:T(8,128)(2,1)S(1)} %lat_rows.3), channel_id=1, source_target_pairs={{0,128},{1,129},{2,130},{3,131},{4,132},{5,133},{6,134},{7,135},{8... | collective-permute-start | bytes 3391496 | tf_op jit(solution)/shard_map/ppermute | solution.py:39
  112.3 5.1 %collective-permute-done.5.below = bf16[2,272,256]{2,1,0:T(8,128)(2,1)S(1)} collective-permute-done((bf16[2,272,256]{2,1,0:T(8,128)(2,1)S(1)}, bf16[2,272,256]{2,1,0:T(8,128)(2,1)S(1)}, u32[]{:S(2)}, u32[]{:S(2)}) %collective-permute-start.5) | collective-permute-done | bytes 278560 | tf_op jit(solution)/shard_map/ppermute | solution.py:39
  117.4 1.4 lat_rows.2
  118.8 2.1 %collective-permute-start.6 = (bf16[272,8,256]{2,1,0:T(8,128)(2,1)S(1)}, bf16[272,8,256]{2,1,0:T(8,128)(2,1)S(1)}, u32[]{:S(2)}, u32[]{:S(2)}) collective-permute-start(bf16[272,8,256]{2,1,0:T(8,128)(2,1)S(1)} %lat_rows.2), channel_id=1, source_target_pairs={{0,128},{1,129},{2,130},{3,131},{4,132},{5,133},{6,134},{7,135},{8... | collective-permute-start | bytes 3342344 | tf_op jit(solution)/shard_map/ppermute | solution.py:39
  120.9 14.9 %collective-permute-done.6 = bf16[272,8,256]{2,1,0:T(8,128)(2,1)S(1)} collective-permute-done((bf16[272,8,256]{2,1,0:T(8,128)(2,1)S(1)}, bf16[272,8,256]{2,1,0:T(8,128)(2,1)S(1)}, u32[]{:S(2)}, u32[]{:S(2)}) %collective-permute-start.6) | collective-permute-done | bytes 1114144 | tf_op jit(solution)/shard_map/ppermute | solution.py:39
  136.0 1.9 %fusion = bf16[1,4,137,8,256]{4,3,2,1,0:T(8,128)(2,1)} fusion(bf16[1,4,137,8,256]{4,3,2,1,0:T(8,128)(2,1)S(1)} %bitcast.55, bf16[1,4,137,8,256]{4,3,2,1,0:T(8,128)(2,1)S(1)} %copy-done), kind=kLoop, calls=%fused_computation.1 | loop fusion | flops 4489216 | bytes 6733824 | tf_op jit(solution)/shard_map/convert_element_type | solution.py:241
  (30 shorter events, 0.5 us)
Async XLA Ops:
  2.3 13.5 %copy-start.5 = (s32[1,8,256]{2,1,0:T(8,128)S(1)}, s32[1,8,256]{2,1,0:T(8,128)}, u32[]{:S(2)}) copy-start(s32[1,8,256]{2,1,0:T(8,128)} %param.14) | copy-start | bytes 24580
  2.3 13.5 %copy-start.6 = (s32[1,8,2,6]{1,2,3,0:T(2,128)S(1)}, s32[1,8,2,6]{1,2,3,0:T(2,128)}, u32[]{:S(2)}) copy-start(s32[1,8,2,6]{1,2,3,0:T(2,128)} %param.10) | copy-start | bytes 1156
  2.3 13.5 %collective-permute-start.7 = (bf16[276,8,256]{2,1,0:T(8,128)(2,1)}, bf16[276,8,256]{2,1,0:T(8,128)(2,1)}, u32[]{:S(2)}, u32[]{:S(2)}) collective-permute-start(bf16[276,8,256]{2,1,0:T(8,128)(2,1)} %slice.40), channel_id=1, source_target_pairs={{128,384},{129,385},{130,386},{131,387},{132,388},{133,389},{134,3... | collective-permute-start | bytes 3391496 | tf_op jit(solution)/shard_map/ppermute | solution.py:39
  6.9 50.0 %collective-permute-start.2 = (bf16[8,272,256]{2,1,0:T(8,128)(2,1)S(1)}, bf16[8,272,256]{2,1,0:T(8,128)(2,1)S(1)}, u32[]{:S(2)}, u32[]{:S(2)}) collective-permute-start(bf16[8,272,256]{2,1,0:T(8,128)(2,1)S(1)} %get-tuple-element.17.refs_3_.refs_8_), channel_id=1, source_target_pairs={{0,1},{1,2},{2,3},{3,4},{4,5},{5,6},{6,7},{7,8},{8,9},{9,10},{10,1... | collective-permute-start | bytes 3342344 | tf_op jit(solution)/shard_map/ppermute | solution.py:39
  10.3 42.5 %collective-permute-start = (bf16[8,272,128]{2,1,0:T(8,128)(2,1)}, bf16[8,272,128]{2,1,0:T(8,128)(2,1)S(1)}, u32[]{:S(2)}, u32[]{:S(2)}) collective-permute-start(bf16[8,272,128]{2,1,0:T(8,128)(2,1)} %get-tuple-element.15), channel_id=1, source_target_pairs={{0,2},{1,3},{2,4},{3,5},{4,6},{5,7},{6,8},{7,9},{8,10},{9,11},{10,... | collective-permute-start | bytes 1671176 | tf_op jit(solution)/shard_map/ppermute | solution.py:39
  17.2 3.6 %copy-start.3 = (s32[1,8,256]{2,1,0:T(8,128)S(1)}, s32[1,8,256]{2,1,0:T(8,128)}, u32[]{:S(2)}) copy-start(s32[1,8,256]{2,1,0:T(8,128)} %param.12) | copy-start | bytes 24580
  17.3 3.6 %copy-start.4 = (s32[1,8,256]{2,1,0:T(8,128)S(1)}, s32[1,8,256]{2,1,0:T(8,128)}, u32[]{:S(2)}) copy-start(s32[1,8,256]{2,1,0:T(8,128)} %param.11) | copy-start | bytes 24580
  17.3 3.7 %copy-start.1 = (f32[1,8,256]{2,1,0:T(8,128)S(1)}, f32[1,8,256]{2,1,0:T(8,128)}, u32[]{:S(2)}) copy-start(f32[1,8,256]{2,1,0:T(8,128)} %param.15) | copy-start | bytes 24580
  17.3 3.7 %copy-start.2 = (f32[1,8,256]{2,1,0:T(8,128)S(1)}, f32[1,8,256]{2,1,0:T(8,128)}, u32[]{:S(2)}) copy-start(f32[1,8,256]{2,1,0:T(8,128)} %param.13) | copy-start | bytes 24580
  17.9 71.4 %collective-permute-start.10 = (bf16[8,288,256]{2,1,0:T(8,128)(2,1)S(1)}, bf16[8,288,256]{2,1,0:T(8,128)(2,1)S(1)}, u32[]{:S(2)}, u32[]{:S(2)}) collective-permute-start(bf16[8,288,256]{2,1,0:T(8,128)(2,1)S(1)} %get-tuple-element.22.refs_3_.refs_8_), channel_id=1, source_target_pairs={{0,1},{1,2},{2,3},{3,4},{4,5},{5,6},{6,7},{7,8},{8,9},{9,10},{10,1... | collective-permute-start | bytes 3538952 | tf_op jit(solution)/shard_map/ppermute | solution.py:39
  21.0 3.7 %collective-permute-start.3 = (f32[4,8,256]{2,1,0:T(8,128)S(1)}, f32[4,8,256]{2,1,0:T(8,128)S(1)}, u32[]{:S(2)}, u32[]{:S(2)}) collective-permute-start(f32[4,8,256]{2,1,0:T(8,128)S(1)} %pad_maximum_fusion.1), channel_id=1, source_target_pairs={{128,384},{129,385},{130,386},{131,387},{132,388},{133,389},{134,3... | collective-permute-start | bytes 98312 | tf_op jit(solution)/shard_map/ppermute | solution.py:39
  21.7 35.2 %collective-permute-start.1 = (bf16[8,272,128]{2,1,0:T(8,128)(2,1)S(1)}, bf16[8,272,128]{2,1,0:T(8,128)(2,1)S(1)}, u32[]{:S(2)}, u32[]{:S(2)}) collective-permute-start(bf16[8,272,128]{2,1,0:T(8,128)(2,1)S(1)} %get-tuple-element.16), channel_id=1, source_target_pairs={{0,31},{1,0},{2,1},{3,2},{4,3},{5,4},{6,5},{7,6},{8,7},{9,8},{10,9... | collective-permute-start | bytes 1671176 | tf_op jit(solution)/shard_map/ppermute | solution.py:39
  24.7 64.6 %collective-permute-start.8 = (bf16[8,288,128]{2,1,0:T(8,128)(2,1)S(1)}, bf16[8,288,128]{2,1,0:T(8,128)(2,1)S(1)}, u32[]{:S(2)}, u32[]{:S(2)}) collective-permute-start(bf16[8,288,128]{2,1,0:T(8,128)(2,1)S(1)} %get-tuple-element.20), channel_id=1, source_target_pairs={{0,2},{1,3},{2,4},{3,5},{4,6},{5,7},{6,8},{7,9},{8,10},{9,11},{10,... | collective-permute-start | bytes 1769480 | tf_op jit(solution)/shard_map/ppermute | solution.py:39
  52.8 36.6 %collective-permute-start.9 = (bf16[8,288,128]{2,1,0:T(8,128)(2,1)S(1)}, bf16[8,288,128]{2,1,0:T(8,128)(2,1)S(1)}, u32[]{:S(2)}, u32[]{:S(2)}) collective-permute-start(bf16[8,288,128]{2,1,0:T(8,128)(2,1)S(1)} %get-tuple-element.21), channel_id=1, source_target_pairs={{0,31},{1,0},{2,1},{3,2},{4,3},{5,4},{6,5},{7,6},{8,7},{9,8},{10,9... | collective-permute-start | bytes 1769480 | tf_op jit(solution)/shard_map/ppermute | solution.py:39
  90.2 16.7 %collective-permute-start.11 = (bf16[2,288,256]{2,1,0:T(8,128)(2,1)S(1)}, bf16[2,288,256]{2,1,0:T(8,128)(2,1)S(1)}, u32[]{:S(2)}, u32[]{:S(2)}) collective-permute-start(bf16[2,288,256]{2,1,0:T(8,128)(2,1)S(1)} %get-tuple-element.23.bot), channel_id=1, source_target_pairs={{0,32},{1,33},{2,34},{3,35},{4,36},{5,37},{6,38},{7,39},{8,40},{9,... | collective-permute-start | bytes 884744 | tf_op jit(solution)/shard_map/ppermute | solution.py:39
  95.0 14.0 %collective-permute-start.12 = (bf16[2,288,256]{2,1,0:T(8,128)(2,1)S(1)}, bf16[2,288,256]{2,1,0:T(8,128)(2,1)S(1)}, u32[]{:S(2)}, u32[]{:S(2)}) collective-permute-start(bf16[2,288,256]{2,1,0:T(8,128)(2,1)S(1)} %get-tuple-element.24.top), channel_id=1, source_target_pairs={{32,0},{33,1},{34,2},{35,3},{36,4},{37,5},{38,6},{39,7},{40,8},{41... | collective-permute-start | bytes 884744 | tf_op jit(solution)/shard_map/ppermute | solution.py:39
  97.8 14.5 %collective-permute-start.4 = (bf16[2,272,256]{2,1,0:T(8,128)(2,1)S(1)}, bf16[2,272,256]{2,1,0:T(8,128)(2,1)S(1)}, u32[]{:S(2)}, u32[]{:S(2)}) collective-permute-start(bf16[2,272,256]{2,1,0:T(8,128)(2,1)S(1)} %get-tuple-element.18.bot), channel_id=1, source_target_pairs={{0,32},{1,33},{2,34},{3,35},{4,36},{5,37},{6,38},{7,39},{8,40},{9,... | collective-permute-start | bytes 835592 | tf_op jit(solution)/shard_map/ppermute | solution.py:39
  103.8 13.6 %collective-permute-start.5 = (bf16[2,272,256]{2,1,0:T(8,128)(2,1)S(1)}, bf16[2,272,256]{2,1,0:T(8,128)(2,1)S(1)}, u32[]{:S(2)}, u32[]{:S(2)}) collective-permute-start(bf16[2,272,256]{2,1,0:T(8,128)(2,1)S(1)} %get-tuple-element.19.top), channel_id=1, source_target_pairs={{32,0},{33,1},{34,2},{35,3},{36,4},{37,5},{38,6},{39,7},{40,8},{41... | collective-permute-start | bytes 835592 | tf_op jit(solution)/shard_map/ppermute | solution.py:39
  110.4 25.4 %collective-permute-start.13 = (bf16[276,8,256]{2,1,0:T(8,128)(2,1)S(1)}, bf16[276,8,256]{2,1,0:T(8,128)(2,1)S(1)}, u32[]{:S(2)}, u32[]{:S(2)}) collective-permute-start(bf16[276,8,256]{2,1,0:T(8,128)(2,1)S(1)} %lat_rows.3), channel_id=1, source_target_pairs={{0,128},{1,129},{2,130},{3,131},{4,132},{5,133},{6,134},{7,135},{8... | collective-permute-start | bytes 3391496 | tf_op jit(solution)/shard_map/ppermute | solution.py:39
  118.8 17.2 %copy-start = (bf16[1,4,137,8,256]{4,3,2,1,0:T(8,128)(2,1)S(1)}, bf16[1,4,137,8,256]{4,3,2,1,0:T(8,128)(2,1)}, u32[]{:S(2)}) copy-start(bf16[1,4,137,8,256]{4,3,2,1,0:T(8,128)(2,1)} %param.8) | copy-start | bytes 6733828
  118.8 17.0 %collective-permute-start.6 = (bf16[272,8,256]{2,1,0:T(8,128)(2,1)S(1)}, bf16[272,8,256]{2,1,0:T(8,128)(2,1)S(1)}, u32[]{:S(2)}, u32[]{:S(2)}) collective-permute-start(bf16[272,8,256]{2,1,0:T(8,128)(2,1)S(1)} %lat_rows.2), channel_id=1, source_target_pairs={{0,128},{1,129},{2,130},{3,131},{4,132},{5,133},{6,134},{7,135},{8... | collective-permute-start | bytes 3342344 | tf_op jit(solution)/shard_map/ppermute | solution.py:39
where the time goes:
time: 139 us; the launch traced here: 138 us
  waiting for transfers between devices  77 us (55%)
  starting transfers between devices  41.4 us (30%)
  Pallas kernels  11 us (8%)
  local copies, waits for them, and re-layouts  3.75 us (3%)
  other arithmetic  3.69 us (3%)
    ppermute x14, waiting for transfers between devices, move(): return lax.ppermute(value, AXES, pairs)  77 us
    ppermute x14, starting transfers between devices, move(): return lax.ppermute(value, AXES, pairs)  41.4 us
    pallas_call x4, Pallas kernels, lon_rows(): pl.pallas_call(functools.partial(lon_kernel, per_step=len(firsts)), grid=...  4.01 us
    pallas_call x2, Pallas kernels, lat_rows(): pl.pallas_call(lat_kernel, out_shape=jax.ShapeDtypeStruct((depth, rows, c...  2.79 us
  transfers between devices with their start and end apart: 14, of which 5 were waited for; matrix products, arithmetic and copies ran while one was open for 2% of the time, Pallas kernels for 7%

commit v1 on v0

--- a/solution.py
+++ b/solution.py
@@ -9,7 +9,8 @@
 
 BLK = 128
 AXES = ("tm", "lat", "lon")
-VMEM_LIMIT = 16 * 1024 * 1024
+VMEM_LIMIT = 14 * 1024 * 1024
+SHORT = pl.CostEstimate(flops=1000, bytes_accessed=1000, transcendentals=0)
 VMEM = pl.BlockSpec(memory_space=pltpu.VMEM)
 
 
@@ -39,7 +40,8 @@
     return lax.ppermute(value, AXES, pairs)
 
 
-def split_kernel(x_ref, whole_ref, west_ref, east_ref, *wide):
+def split_kernel(x_ref, *refs, picked):
+    whole_ref, west_ref, east_ref, *wide = refs[-5:]
     depth, rows, cols = x_ref.shape
     padded = whole_ref.shape[1]
     for g, (half_ref, buf) in enumerate(zip((west_ref, east_ref), wide)):
@@ -47,30 +49,60 @@
         buf[: depth * rows] = x_ref[:, :, lanes].astype(jnp.float32).reshape(depth * rows, BLK)
         if padded > depth:
             buf[depth * rows :] = jnp.zeros(((padded - depth) * rows, BLK), jnp.float32)
-        for r in range(rows):
+        for i, r in enumerate(picked):
             slab = buf[pl.ds(r, padded, stride=rows), :].astype(jnp.bfloat16)
-            whole_ref[r, :, lanes] = slab
-            half_ref[r] = slab
-
-
-def split_rows(x):
-    _, rows, cols = x.shape
-    depth = -(-x.shape[0] // 16) * 16
-    bf16 = jnp.bfloat16
-    return pl.pallas_call(
-        split_kernel,
-        out_shape=(
-            jax.ShapeDtypeStruct((rows, depth, cols), bf16),
-            jax.ShapeDtypeStruct((rows, depth, cols // 2), bf16),
-            jax.ShapeDtypeStruct((rows, depth, cols // 2), bf16),
-        ),
-        in_specs=[VMEM],
+            whole_ref[i, :, lanes] = slab
+            half_ref[i] = slab
+
+
+def split_rows(x, picked, padded, after=()):
+    depth, rows, cols = x.shape
+    n = len(picked)
+    half = jax.ShapeDtypeStruct((n, padded, cols // 2), x.dtype)
+    return pl.pallas_call(
+        functools.partial(split_kernel, picked=picked),
+        out_shape=(jax.ShapeDtypeStruct((n, padded, cols), x.dtype), half, half),
+        in_specs=[VMEM] + [pl.BlockSpec(memory_space=pl.ANY)] * len(after),
         out_specs=(VMEM, VMEM, VMEM),
-        scratch_shapes=[pltpu.VMEM((depth * rows, BLK), jnp.float32)] * 2,
-        compiler_params=params(),
-        cost_estimate=pl.CostEstimate(flops=0, bytes_accessed=6 * x.size, transcendentals=0),
+        scratch_shapes=[pltpu.VMEM((padded * rows, BLK), jnp.float32)] * 2,
+        compiler_params=params(),
+        cost_estimate=SHORT,
         name="split_rows",
-    )(x)
+    )(x, *after)
+
+
+def choose_kernel(lent_flag, lent_ref, own_ref, own_east_ref, *refs):
+    whole_ref, west_ref, east_ref = refs[-3:]
+    half = west_ref.shape[2]
+    east_ref[...] = own_east_ref[...]
+
+    def put(ref):
+        for r in range(whole_ref.shape[0]):
+            slab = ref[r]
+            whole_ref[r] = slab
+            west_ref[r] = slab[:, :half]
+
+    @pl.when(lent_flag[0] == 1)
+    def _():
+        put(lent_ref)
+
+    @pl.when(lent_flag[0] == 0)
+    def _():
+        put(own_ref)
+
+
+def choose(flag, lent, own, own_east, after):
+    half = jax.ShapeDtypeStruct(own_east.shape, own.dtype)
+    return pl.pallas_call(
+        choose_kernel,
+        out_shape=(jax.ShapeDtypeStruct(own.shape, own.dtype), half, half),
+        in_specs=[pl.BlockSpec(memory_space=pltpu.SMEM), VMEM, VMEM, VMEM]
+        + [pl.BlockSpec(memory_space=pl.ANY)] * len(after),
+        out_specs=(VMEM, VMEM, VMEM),
+        compiler_params=params(),
+        cost_estimate=SHORT,
+        name="choose",
+    )(flag, lent, own, own_east, *after)
 
 
 def matrix_kernel(geo_ref, m_ref):
@@ -96,9 +128,7 @@
         in_specs=[pl.BlockSpec(geo.shape, lambda r: (0, 0, 0))],
         out_specs=pl.BlockSpec((1, span, cols), lambda r: (r, 0, 0)),
         compiler_params=params(),
-        cost_estimate=pl.CostEstimate(
-            flops=9 * rows * span * cols, bytes_accessed=2 * rows * span * cols, transcendentals=0
-        ),
+        cost_estimate=SHORT,
         name="matrices",
     )(geo)
 
@@ -113,35 +143,35 @@
     return total.astype(jnp.bfloat16)
 
 
-def lon_kernel(*refs, per_step):
-    ins, outs = refs[: 5 * per_step], refs[len(refs) - per_step :]
+def lon_kernel(lent_flag, *refs, per_step):
+    ins, outs = refs[: 6 * per_step], refs[len(refs) - per_step :]
+    lent = lent_flag[0] == 1
     for k in range(per_step):
-        far, near, west, own, m = ins[5 * k : 5 * k + 5]
-        outs[k][0] = row_product(far[0], near[0], west[0], own[0], m[0])
-
-
-def lon_rows(far, near, west, own, m, firsts, count, after=()):
+        far, far_lent, near, west, own, m = ins[6 * k : 6 * k + 6]
+        second_west = jnp.where(lent, far_lent[0], far[0])
+        outs[k][0] = row_product(second_west, near[0], west[0], own[0], m[0])
+
+
+def lon_rows(flag, far, far_lent, near, west, own, m, firsts, count, after=()):
     _, depth, cols = own.shape
-    arrays = (far, near, west, own, m)
+    arrays = (far, far_lent, near, west, own)
 
     def at(array, first):
         return pl.BlockSpec((1,) + array.shape[1:], lambda i, first=first: (i + first, 0, 0))
 
+    specs = []
+    for slab, row in firsts:
+        specs += [at(array, slab) for array in arrays] + [at(m, row)]
     return pl.pallas_call(
         functools.partial(lon_kernel, per_step=len(firsts)),
         grid=(count,),
         out_shape=[jax.ShapeDtypeStruct((count, depth, cols), jnp.bfloat16) for _ in firsts],
-        in_specs=[at(array, first) for first in firsts for array in arrays]
-        + [pl.BlockSpec(memory_space=pl.ANY)] * len(after),
+        in_specs=[pl.BlockSpec(memory_space=pltpu.SMEM)] + specs + [pl.BlockSpec(memory_space=pl.ANY)] * len(after),
         out_specs=[pl.BlockSpec((1, depth, cols), lambda i: (i, 0, 0)) for _ in firsts],
         compiler_params=params(),
-        cost_estimate=pl.CostEstimate(
-            flops=2 * len(firsts) * count * depth * m.shape[1] * cols,
-            bytes_accessed=2 * len(firsts) * count * (4 * depth * cols + m.shape[1] * cols),
-            transcendentals=0,
-        ),
+        cost_estimate=SHORT,
         name="lon_rows",
-    )(*(arrays * len(firsts)), *after)
+    )(flag, *((*arrays, m) * len(firsts)), *after)
 
 
 def lat_kernel(above, top, mid, bot, below, geo_ref, out_ref, *wide):
@@ -180,9 +210,7 @@
         out_specs=VMEM,
         scratch_shapes=[pltpu.VMEM((depth * rows, BLK), jnp.float32)] * (cols // BLK),
         compiler_params=params(),
-        cost_estimate=pl.CostEstimate(
-            flops=10 * depth * rows * cols, bytes_accessed=5 * depth * rows * cols, transcendentals=0
-        ),
+        cost_estimate=SHORT,
         name="lat_rows",
     )(above, top, mid, bot, below, geo)
 
@@ -207,37 +235,47 @@
 def body(state, *rest):
     fields_n, levels, rows, cols = state.shape[1:]
     depth = fields_n * levels
-    windows, bands, tiles = (lax.axis_size(a) for a in AXES)
+    padded = -(-depth // 8) * 8
+    _, bands, tiles = (lax.axis_size(a) for a in AXES)
     flat = state.reshape(depth, rows, cols)
-    cut = depth // 32 * 16
     tm = lax.axis_index("tm")
+    flag = (tm == 3).astype(jnp.int32).reshape(1)
+
+    active = (0, 2, 3)
 
     def lend(t, b, j):
         return (3, b, j)
 
+    def along_lon(steps):
+        return lambda t, b, j: (t, b, (j + steps) % tiles)
+
     geo_own = geometry(*rest)
     geo = jnp.where(tm == 3, move(geo_own, lend, (1,)), geo_own)
-    second = jnp.where(tm == 3, move(flat[cut:], lend, (1,)), flat[cut:])
     m = matrices(geo, 3 * cols)
 
-    ends, after = [], ()
-    parts = (
-        (flat[:cut], (0, 1, 2), {0: 1, 1: 2, 2: 3}),
-        (second, (0, 2, 3), {0: 1, 3: 2, 2: 3}),
-    )
-    for part, active, onward in parts:
-        own, west_half, east_half = split_rows(part)
-        west = move(own, lambda t, b, j: (t, b, (j + 1) % tiles), active)
-        near = move(west_half, lambda t, b, j: (t, b, (j - 1) % tiles), active)
-        far = move(east_half, lambda t, b, j: (t, b, (j + 2) % tiles), active)
-        top, bot = lon_rows(far, near, west, own, m, (0, rows - 2), 2, after)
-        above = move(bot, lambda t, b, j: (t, b + 1, j) if b + 1 < bands else None, active)
-        below = move(top, lambda t, b, j: (t, b - 1, j) if b > 0 else None, active)
-        (mid,) = lon_rows(far, near, west, own, m, (2,), rows - 4)
-        after = (mid,)
-        end = lat_rows(above, top, mid, bot, below, geo, part.shape[0])
-        ends.append(move(end, lambda t, b, j: (onward[t], b, j), active))
-    previous = jnp.concatenate(ends, axis=0)
+    def neighbours(own, west_half):
+        return move(own, along_lon(1), active), move(west_half, along_lon(-1), active)
+
+    edge, inner = (0, 1, rows - 2, rows - 1), tuple(range(2, rows - 2))
+    raw, _, east = split_rows(flat, edge, padded)
+    far = move(east, along_lon(2), (0, 1, 2))
+    own, west_half, _ = choose(flag, move(raw, lend, (1,)), raw, east, ())
+    west, near = neighbours(own, west_half)
+    raw_in, _, east_in = split_rows(flat, inner, padded, (own,))
+    lent_in = move(raw_in, lend, (1,))
+    own_in, west_half_in, east_in = choose(flag, lent_in, raw_in, east_in, (near, geo))
+    far_in = move(east_in, along_lon(2), (0, 1, 2))
+    west_in, near_in = neighbours(own_in, west_half_in)
+
+    far_lent = move(far, lend, (1,))
+    top, bot = lon_rows(flag, far, far_lent, near, west, own, m, ((0, 0), (2, rows - 2)), 2)
+    above = move(bot, lambda t, b, j: (t, b + 1, j) if b + 1 < bands else None, active)
+    below = move(top, lambda t, b, j: (t, b - 1, j) if b > 0 else None, active)
+    behind, above = lax.optimization_barrier((far_in, above))
+    far_lent_in = move(behind, lend, (1,))
+    (mid,) = lon_rows(flag, far_in, far_lent_in, near_in, west_in, own_in, m, ((0, 2),), rows - 4, (top,))
+    end = lat_rows(above, top, mid, bot, below, geo, depth)
+    previous = move(end, lambda t, b, j: ({0: 1, 2: 3, 3: 2}[t], b, j), active)
     misfit = (flat.astype(jnp.float32) - previous.astype(jnp.float32)).astype(jnp.bfloat16)
     return misfit.reshape(state.shape)
 

time: 139 us -> 112 us (0.81)
  the two profiles are of different devices: /device:TPU:26 before, /device:TPU:211 now
where the time goes in v1:
time: 112 us; the launch traced here: 111 us
  waiting for transfers between devices  54 us (48%)
  starting transfers between devices  32.5 us (29%)
  Pallas kernels  16.8 us (15%)
  local copies, waits for them, and re-layouts  4.82 us (4%)
  other arithmetic  2.25 us (2%)
    ppermute x14, waiting for transfers between devices, move(): return lax.ppermute(value, AXES, pairs)  54 us
    ppermute x14, starting transfers between devices, move(): return lax.ppermute(value, AXES, pairs)  32.5 us
    unnamed x26, local copies, waits for them, and re-layouts  4.74 us
    pallas_call x2, Pallas kernels, choose(): pl.pallas_call(choose_kernel, out_shape=(jax.ShapeDtypeStruct(own.shape,...  4.17 us
    pallas_call x2, Pallas kernels, lon_rows(): pl.pallas_call(functools.partial(lon_kernel, per_step=len(firsts)), grid=...  4.15 us
    pallas_call x2, Pallas kernels, split_rows(): pl.pallas_call(functools.partial(split_kernel, picked=picked), out_shape=...  3.53 us
    pallas_call x1, Pallas kernels, lat_rows(): pl.pallas_call(lat_kernel, out_shape=jax.ShapeDtypeStruct((depth, rows, c...  2.85 us
  transfers between devices with their start and end apart: 14, of which 5 were waited for; matrix products, arithmetic and copies ran while one was open for 0% of the time, Pallas kernels for 11%

profile of v1, /device:TPU:211, one launch (start us, length us, event | category | flops | bytes accessed | tf_op | source)
XLA Modules:
  0.0 111.4 jit_solution(13303338251205821669)
XLA Ops:
  0.0 1.6 %copy-done = bf16[1,4,137,8,256]{4,3,2,1,0:T(8,128)(2,1)S(1)} copy-done((bf16[1,4,137,8,256]{4,3,2,1,0:T(8,128)(2,1)S(1)}, bf16[1,4,137,8,256]{4,3,2,1,0:T(8,128)(2,1)}, u32[]{:S(2)}) %copy-start) | copy-done | bytes 2244632
  1.6 1.7 %split_rows.2 = (bf16[4,552,256]{2,1,0:T(8,128)(2,1)S(1)}, bf16[4,552,128]{2,1,0:T(8,128)(2,1)}, bf16[4,552,128]{2,1,0:T(8,128)(2,1)}) custom-call(bf16[548,8,256]{2,1,0:T(8,128)(2,1)S(1)} %bitcast.53), custom_call_target="tpu_custom_call" | custom-call | flops 1000 | bytes 1000 | tf_op jit(solution)/shard_map/split_rows/pallas_call | solution.py:62
  3.3 4.2 %collective-permute-start = (bf16[4,552,256]{2,1,0:T(8,128)(2,1)S(1)}, bf16[4,552,256]{2,1,0:T(8,128)(2,1)}, u32[]{:S(2)}, u32[]{:S(2)}) collective-permute-start(bf16[4,552,256]{2,1,0:T(8,128)(2,1)S(1)} %get-tuple-element.18.own_ref), channel_id=1, source_target_pairs={{128,384},{129,385},{130,386},{131,387},{132,388},{133,389},{134,3... | collective-permute-start | bytes 3391496 | tf_op jit(solution)/shard_map/ppermute | solution.py:40
  7.5 1.0 copy-done.2
  8.5 3.7 %collective-permute-start.5 = (bf16[4,552,128]{2,1,0:T(8,128)(2,1)}, bf16[4,552,128]{2,1,0:T(8,128)(2,1)}, u32[]{:S(2)}, u32[]{:S(2)}) collective-permute-start(bf16[4,552,128]{2,1,0:T(8,128)(2,1)} %get-tuple-element.19.own_east_ref), channel_id=1, source_target_pairs={{0,2},{1,3},{2,4},{3,5},{4,6},{5,7},{6,8},{7,9},{8,10},{9,11},{10,... | collective-permute-start | bytes 1695752 | tf_op jit(solution)/shard_map/ppermute | solution.py:40
  12.3 6.8 %collective-permute-done.lent_ref = bf16[4,552,256]{2,1,0:T(8,128)(2,1)} collective-permute-done((bf16[4,552,256]{2,1,0:T(8,128)(2,1)S(1)}, bf16[4,552,256]{2,1,0:T(8,128)(2,1)}, u32[]{:S(2)}, u32[]{:S(2)}) %collective-permute-start) | collective-permute-done | bytes 1130528 | tf_op jit(solution)/shard_map/ppermute | solution.py:40
  19.1 1.3 %copy-done.3 = bf16[4,552,256]{2,1,0:T(8,128)(2,1)S(1)} copy-done((bf16[4,552,256]{2,1,0:T(8,128)(2,1)S(1)}, bf16[4,552,256]{2,1,0:T(8,128)(2,1)}, u32[]{:S(2)}) %copy-start.3) | copy-done | bytes 1130520
  20.4 2.4 %choose.2 = (bf16[4,552,256]{2,1,0:T(8,128)(2,1)S(1)}, bf16[4,552,128]{2,1,0:T(8,128)(2,1)S(1)}, bf16[4,552,128]{2,1,0:T(8,128)(2,1)}) custom-call(s32[1]{0:T(128)} %bitcast.1.lent_flag, bf16[4,552,256]{2,1,0:T(8,128)(2,1)} %collective-permute-done.lent_ref, bf16[4,552,256]{2,1,0:T(8,128)(2,1)S(1)} %copy-done.3, ...), custom_call_target="tpu_custom_call" | custom-call | flops 1000 | bytes 1000 | tf_op jit(solution)/shard_map/choose/pallas_call | solution.py:96
  22.8 1.9 %split_rows.3 = (bf16[4,552,256]{2,1,0:T(8,128)(2,1)}, bf16[4,552,128]{2,1,0:T(8,128)(2,1)}, bf16[4,552,128]{2,1,0:T(8,128)(2,1)S(1)}) custom-call(bf16[548,8,256]{2,1,0:T(8,128)(2,1)S(1)} %bitcast.54, bf16[4,552,256]{2,1,0:T(8,128)(2,1)S(1)} %get-tuple-element.20.refs_0_.refs_4_.refs_10_), custom_call_target="tpu_custom_call" | custom-call | flops 1000 | bytes 1000 | tf_op jit(solution)/shard_map/split_rows/pallas_call | solution.py:62
  24.7 0.8 copy-done.4
  25.5 5.2 %collective-permute-start.1 = (bf16[4,552,256]{2,1,0:T(8,128)(2,1)}, bf16[4,552,256]{2,1,0:T(8,128)(2,1)}, u32[]{:S(2)}, u32[]{:S(2)}) collective-permute-start(bf16[4,552,256]{2,1,0:T(8,128)(2,1)} %get-tuple-element.21.own_ref), channel_id=1, source_target_pairs={{128,384},{129,385},{130,386},{131,387},{132,388},{133,389},{134,3... | collective-permute-start | bytes 3391496 | tf_op jit(solution)/shard_map/ppermute | solution.py:40
  30.7 1.7 %collective-permute-start.7 = (bf16[4,552,256]{2,1,0:T(8,128)(2,1)S(1)}, bf16[4,552,256]{2,1,0:T(8,128)(2,1)}, u32[]{:S(2)}, u32[]{:S(2)}) collective-permute-start(bf16[4,552,256]{2,1,0:T(8,128)(2,1)S(1)} %get-tuple-element.20.refs_0_.refs_4_.refs_10_), channel_id=1, source_target_pairs={{0,1},{1,2},{2,3},{3,4},{4,5},{5,6},{6,7},{7,8},{8,9},{9,10},{10,1... | collective-permute-start | bytes 3391496 | tf_op jit(solution)/shard_map/ppermute | solution.py:40
  33.2 1.6 %collective-permute-start.6 = (bf16[4,552,128]{2,1,0:T(8,128)(2,1)}, bf16[4,552,128]{2,1,0:T(8,128)(2,1)S(1)}, u32[]{:S(2)}, u32[]{:S(2)}) collective-permute-start(bf16[4,552,128]{2,1,0:T(8,128)(2,1)} %collective-permute-done.5.refs_0_.refs_6_), channel_id=1, source_target_pairs={{128,384},{129,385},{130,386},{131,387},{132,388},{133,389},{134,3... | collective-permute-start | bytes 1695752 | tf_op jit(solution)/shard_map/ppermute | solution.py:40
  34.8 0.7 collective-permute-start.2
  35.7 3.0 %collective-permute-start.3 = (f32[4,8,256]{2,1,0:T(8,128)S(1)}, f32[4,8,256]{2,1,0:T(8,128)S(1)}, u32[]{:S(2)}, u32[]{:S(2)}) collective-permute-start(f32[4,8,256]{2,1,0:T(8,128)S(1)} %pad_maximum_fusion), channel_id=1, source_target_pairs={{128,384},{129,385},{130,386},{131,387},{132,388},{133,389},{134,3... | collective-permute-start | bytes 98312 | tf_op jit(solution)/shard_map/ppermute | solution.py:40
  38.7 10.2 %collective-permute-done.3 = f32[4,8,256]{2,1,0:T(8,128)S(1)} collective-permute-done((f32[4,8,256]{2,1,0:T(8,128)S(1)}, f32[4,8,256]{2,1,0:T(8,128)S(1)}, u32[]{:S(2)}, u32[]{:S(2)}) %collective-permute-start.3) | collective-permute-done | bytes 32800 | tf_op jit(solution)/shard_map/ppermute | solution.py:40
  48.9 2.1 %matrices.1.refs_5_.refs_11_ = bf16[8,768,256]{2,1,0:T(8,128)(2,1)S(1)} custom-call(f32[4,8,256]{2,1,0:T(8,128)S(1)} %broadcast_select_fusion.refs_1_.geo_ref), custom_call_target="tpu_custom_call" | custom-call | flops 1000 | bytes 1000 | tf_op jit(solution)/shard_map/matrices/pallas_call | solution.py:124
  51.1 1.8 %choose.3 = (bf16[4,552,256]{2,1,0:T(8,128)(2,1)S(1)}, bf16[4,552,128]{2,1,0:T(8,128)(2,1)S(1)}, bf16[4,552,128]{2,1,0:T(8,128)(2,1)S(1)}) custom-call(s32[1]{0:T(128)} %bitcast.1.lent_flag, bf16[4,552,256]{2,1,0:T(8,128)(2,1)} %collective-permute-done.1.lent_ref, bf16[4,552,256]{2,1,0:T(8,128)(2,1)} %get-tuple-element.21.own_ref, ...), custom_call_target="tpu_custom_call" | custom-call | flops 1000 | bytes 1000 | tf_op jit(solution)/shard_map/choose/pallas_call | solution.py:96
  52.9 3.5 %collective-permute-start.4 = (bf16[4,552,128]{2,1,0:T(8,128)(2,1)S(1)}, bf16[4,552,128]{2,1,0:T(8,128)(2,1)S(1)}, u32[]{:S(2)}, u32[]{:S(2)}) collective-permute-start(bf16[4,552,128]{2,1,0:T(8,128)(2,1)S(1)} %get-tuple-element.24), channel_id=1, source_target_pairs={{0,2},{1,3},{2,4},{3,5},{4,6},{5,7},{6,8},{7,9},{8,10},{9,11},{10,... | collective-permute-start | bytes 1695752 | tf_op jit(solution)/shard_map/ppermute | solution.py:40
  56.4 2.5 %lon_rows.2 = (bf16[2,552,256]{2,1,0:T(8,128)(2,1)S(1)}, bf16[2,552,256]{2,1,0:T(8,128)(2,1)S(1)}) custom-call(s32[1]{0:T(128)} %bitcast.1.lent_flag, bf16[4,552,128]{2,1,0:T(8,128)(2,1)} %collective-permute-done.5.refs_0_.refs_6_, bf16[4,552,128]{2,1,0:T(8,128)(2,1)S(1)} %collective-permute-done.6.refs_1_.refs_7_, ...), custom_call_target="tpu_custom_call" | custom-call | flops 1000 | bytes 1000 | tf_op jit(solution)/shard_map/lon_rows/pallas_call | solution.py:165
  58.9 0.7 collective-permute-start.8
  59.6 0.7 collective-permute-start.11
  60.4 0.7 collective-permute-start.10
  61.1 11.3 %collective-permute-done.4.refs_0_ = bf16[4,552,128]{2,1,0:T(8,128)(2,1)S(1)} collective-permute-done((bf16[4,552,128]{2,1,0:T(8,128)(2,1)S(1)}, bf16[4,552,128]{2,1,0:T(8,128)(2,1)S(1)}, u32[]{:S(2)}, u32[]{:S(2)}) %collective-permute-start.4) | collective-permute-done | bytes 565280 | tf_op jit(solution)/shard_map/ppermute | solution.py:40
  72.4 4.7 %collective-permute-start.9 = (bf16[4,552,128]{2,1,0:T(8,128)(2,1)S(1)}, bf16[4,552,128]{2,1,0:T(8,128)(2,1)S(1)}, u32[]{:S(2)}, u32[]{:S(2)}) collective-permute-start(bf16[4,552,128]{2,1,0:T(8,128)(2,1)S(1)} %collective-permute-done.4.refs_0_), channel_id=1, source_target_pairs={{128,384},{129,385},{130,386},{131,387},{132,388},{133,389},{134,3... | collective-permute-start | bytes 1695752 | tf_op jit(solution)/shard_map/ppermute | solution.py:40
  77.2 0.7 collective-permute-start.12
  77.9 5.8 %collective-permute-done.9.refs_1_ = bf16[4,552,128]{2,1,0:T(8,128)(2,1)S(1)} collective-permute-done((bf16[4,552,128]{2,1,0:T(8,128)(2,1)S(1)}, bf16[4,552,128]{2,1,0:T(8,128)(2,1)S(1)}, u32[]{:S(2)}, u32[]{:S(2)}) %collective-permute-start.9) | collective-permute-done | bytes 565280 | tf_op jit(solution)/shard_map/ppermute | solution.py:40
  83.7 1.6 %lon_rows.3.mid = bf16[4,552,256]{2,1,0:T(8,128)(2,1)S(1)} custom-call(s32[1]{0:T(128)} %bitcast.1.lent_flag, bf16[4,552,128]{2,1,0:T(8,128)(2,1)S(1)} %collective-permute-done.4.refs_0_, bf16[4,552,128]{2,1,0:T(8,128)(2,1)S(1)} %collective-permute-done.9.refs_1_, bf16[4,552,128]{2,1,0:T(8,128)(2,1)S(1)} %collective-permute-done.10.refs_2_, ...), custom_call_target="tpu_custom_call" | custom-call | flops 1000 | bytes 1000 | tf_op jit(solution)/shard_map/lon_rows/pallas_call | solution.py:165
  85.3 2.9 %lat_rows.1 = bf16[548,8,256]{2,1,0:T(8,128)(2,1)S(1)} custom-call(bf16[2,552,256]{2,1,0:T(8,128)(2,1)S(1)} %collective-permute-done.8.above, bf16[2,552,256]{2,1,0:T(8,128)(2,1)S(1)} %get-tuple-element.27.refs_6_.top, bf16[4,552,256]{2,1,0:T(8,128)(2,1)S(1)} %lon_rows.3.mid, bf16[2,552,256]{2,1,0:T(8,128)(2,1)S(1)} %get-tuple-element.25.bot, ...), custom_call_target="tpu_custom_call" | custom-call | flops 1000 | bytes 1000 | tf_op jit(solution)/shard_map/lat_rows/pallas_call | solution.py:206
  88.2 1.3 %collective-permute-start.13 = (bf16[548,8,256]{2,1,0:T(8,128)(2,1)S(1)}, bf16[548,8,256]{2,1,0:T(8,128)(2,1)S(1)}, u32[]{:S(2)}, u32[]{:S(2)}) collective-permute-start(bf16[548,8,256]{2,1,0:T(8,128)(2,1)S(1)} %lat_rows.1), channel_id=1, source_target_pairs={{0,128},{1,129},{2,130},{3,131},{4,132},{5,133},{6,134},{7,135},{8... | collective-permute-start | bytes 6733832 | tf_op jit(solution)/shard_map/ppermute | solution.py:40
  89.5 19.8 %collective-permute-done.13 = bf16[548,8,256]{2,1,0:T(8,128)(2,1)S(1)} collective-permute-done((bf16[548,8,256]{2,1,0:T(8,128)(2,1)S(1)}, bf16[548,8,256]{2,1,0:T(8,128)(2,1)S(1)}, u32[]{:S(2)}, u32[]{:S(2)}) %collective-permute-start.13) | collective-permute-done | bytes 2244640 | tf_op jit(solution)/shard_map/ppermute | solution.py:40
  109.3 2.1 %subtract_convert_fusion = bf16[548,8,256]{2,1,0:T(8,128)(2,1)} fusion(bf16[548,8,256]{2,1,0:T(8,128)(2,1)S(1)} %collective-permute-done.13, bf16[1,4,137,8,256]{4,3,2,1,0:T(8,128)(2,1)S(1)} %copy-done.1), kind=kLoop, calls=%fused_computation | loop fusion | flops 4489216 | bytes 6733824 | tf_op jit(solution)/shard_map/convert_element_type | solution.py:279
  (37 shorter events, 0.3 us)
Async XLA Ops:
  0.0 1.6 %copy-start = (bf16[1,4,137,8,256]{4,3,2,1,0:T(8,128)(2,1)S(1)}, bf16[1,4,137,8,256]{4,3,2,1,0:T(8,128)(2,1)}, u32[]{:S(2)}) copy-start(bf16[1,4,137,8,256]{4,3,2,1,0:T(8,128)(2,1)} %param.8) | copy-start | bytes 6733828
  1.6 21.2 %copy-start.1 = (bf16[1,4,137,8,256]{4,3,2,1,0:T(8,128)(2,1)S(1)}, bf16[1,4,137,8,256]{4,3,2,1,0:T(8,128)(2,1)}, u32[]{:S(2)}) copy-start(bf16[1,4,137,8,256]{4,3,2,1,0:T(8,128)(2,1)} %param.8) | copy-start | bytes 6733828
  3.3 15.8 %collective-permute-start = (bf16[4,552,256]{2,1,0:T(8,128)(2,1)S(1)}, bf16[4,552,256]{2,1,0:T(8,128)(2,1)}, u32[]{:S(2)}, u32[]{:S(2)}) collective-permute-start(bf16[4,552,256]{2,1,0:T(8,128)(2,1)S(1)} %get-tuple-element.18.own_ref), channel_id=1, source_target_pairs={{128,384},{129,385},{130,386},{131,387},{132,388},{133,389},{134,3... | collective-permute-start | bytes 3391496 | tf_op jit(solution)/shard_map/ppermute | solution.py:40
  7.5 1.0 copy-start.2
  8.5 24.7 %collective-permute-start.5 = (bf16[4,552,128]{2,1,0:T(8,128)(2,1)}, bf16[4,552,128]{2,1,0:T(8,128)(2,1)}, u32[]{:S(2)}, u32[]{:S(2)}) collective-permute-start(bf16[4,552,128]{2,1,0:T(8,128)(2,1)} %get-tuple-element.19.own_east_ref), channel_id=1, source_target_pairs={{0,2},{1,3},{2,4},{3,5},{4,6},{5,7},{6,8},{7,9},{8,10},{9,11},{10,... | collective-permute-start | bytes 1695752 | tf_op jit(solution)/shard_map/ppermute | solution.py:40
  19.1 1.3 %copy-start.3 = (bf16[4,552,256]{2,1,0:T(8,128)(2,1)S(1)}, bf16[4,552,256]{2,1,0:T(8,128)(2,1)}, u32[]{:S(2)}) copy-start(bf16[4,552,256]{2,1,0:T(8,128)(2,1)} %copy-done.2) | copy-start | bytes 3391492
  22.7 2.7 %copy-start.6 = (bf16[4,552,128]{2,1,0:T(8,128)(2,1)}, bf16[4,552,128]{2,1,0:T(8,128)(2,1)S(1)}, u32[]{:S(2)}) copy-start(bf16[4,552,128]{2,1,0:T(8,128)(2,1)S(1)} %get-tuple-element.23) | copy-start | bytes 1695748
  22.8 10.3 %copy-start.11 = (s32[1,8,256]{2,1,0:T(8,128)S(1)}, s32[1,8,256]{2,1,0:T(8,128)}, u32[]{:S(2)}) copy-start(s32[1,8,256]{2,1,0:T(8,128)} %param.14) | copy-start | bytes 24580
  22.8 10.3 %copy-start.12 = (s32[1,8,2,6]{1,2,3,0:T(2,128)S(1)}, s32[1,8,2,6]{1,2,3,0:T(2,128)}, u32[]{:S(2)}) copy-start(s32[1,8,2,6]{1,2,3,0:T(2,128)} %param.10) | copy-start | bytes 1156
  22.8 12.8 %copy-start.9 = (s32[1,8,256]{2,1,0:T(8,128)S(1)}, s32[1,8,256]{2,1,0:T(8,128)}, u32[]{:S(2)}) copy-start(s32[1,8,256]{2,1,0:T(8,128)} %param.12) | copy-start | bytes 24580
  22.8 12.8 %copy-start.10 = (s32[1,8,256]{2,1,0:T(8,128)S(1)}, s32[1,8,256]{2,1,0:T(8,128)}, u32[]{:S(2)}) copy-start(s32[1,8,256]{2,1,0:T(8,128)} %param.11) | copy-start | bytes 24580
  22.8 12.9 %copy-start.7 = (f32[1,8,256]{2,1,0:T(8,128)S(1)}, f32[1,8,256]{2,1,0:T(8,128)}, u32[]{:S(2)}) copy-start(f32[1,8,256]{2,1,0:T(8,128)} %param.15) | copy-start | bytes 24580
  22.8 12.9 %copy-start.8 = (f32[1,8,256]{2,1,0:T(8,128)S(1)}, f32[1,8,256]{2,1,0:T(8,128)}, u32[]{:S(2)}) copy-start(f32[1,8,256]{2,1,0:T(8,128)} %param.13) | copy-start | bytes 24580
  24.7 0.8 copy-start.4
  25.5 25.6 %collective-permute-start.1 = (bf16[4,552,256]{2,1,0:T(8,128)(2,1)}, bf16[4,552,256]{2,1,0:T(8,128)(2,1)}, u32[]{:S(2)}, u32[]{:S(2)}) collective-permute-start(bf16[4,552,256]{2,1,0:T(8,128)(2,1)} %get-tuple-element.21.own_ref), channel_id=1, source_target_pairs={{128,384},{129,385},{130,386},{131,387},{132,388},{133,389},{134,3... | collective-permute-start | bytes 3391496 | tf_op jit(solution)/shard_map/ppermute | solution.py:40
  30.7 25.7 %collective-permute-start.7 = (bf16[4,552,256]{2,1,0:T(8,128)(2,1)S(1)}, bf16[4,552,256]{2,1,0:T(8,128)(2,1)}, u32[]{:S(2)}, u32[]{:S(2)}) collective-permute-start(bf16[4,552,256]{2,1,0:T(8,128)(2,1)S(1)} %get-tuple-element.20.refs_0_.refs_4_.refs_10_), channel_id=1, source_target_pairs={{0,1},{1,2},{2,3},{3,4},{4,5},{5,6},{6,7},{7,8},{8,9},{9,10},{10,1... | collective-permute-start | bytes 3391496 | tf_op jit(solution)/shard_map/ppermute | solution.py:40
  33.1 18.0 %copy-start.5 = (bf16[4,552,128]{2,1,0:T(8,128)(2,1)S(1)}, bf16[4,552,128]{2,1,0:T(8,128)(2,1)}, u32[]{:S(2)}) copy-start(bf16[4,552,128]{2,1,0:T(8,128)(2,1)} %copy-done.4) | copy-start | bytes 1695748
  33.2 23.2 %collective-permute-start.6 = (bf16[4,552,128]{2,1,0:T(8,128)(2,1)}, bf16[4,552,128]{2,1,0:T(8,128)(2,1)S(1)}, u32[]{:S(2)}, u32[]{:S(2)}) collective-permute-start(bf16[4,552,128]{2,1,0:T(8,128)(2,1)} %collective-permute-done.5.refs_0_.refs_6_), channel_id=1, source_target_pairs={{128,384},{129,385},{130,386},{131,387},{132,388},{133,389},{134,3... | collective-permute-start | bytes 1695752 | tf_op jit(solution)/shard_map/ppermute | solution.py:40
  34.8 16.3 %collective-permute-start.2 = (bf16[4,552,128]{2,1,0:T(8,128)(2,1)}, bf16[4,552,128]{2,1,0:T(8,128)(2,1)S(1)}, u32[]{:S(2)}, u32[]{:S(2)}) collective-permute-start(bf16[4,552,128]{2,1,0:T(8,128)(2,1)} %copy-done.6), channel_id=1, source_target_pairs={{0,31},{1,0},{2,1},{3,2},{4,3},{5,4},{6,5},{7,6},{8,7},{9,8},{10,9... | collective-permute-start | bytes 1695752 | tf_op jit(solution)/shard_map/ppermute | solution.py:40
  35.7 13.2 %collective-permute-start.3 = (f32[4,8,256]{2,1,0:T(8,128)S(1)}, f32[4,8,256]{2,1,0:T(8,128)S(1)}, u32[]{:S(2)}, u32[]{:S(2)}) collective-permute-start(f32[4,8,256]{2,1,0:T(8,128)S(1)} %pad_maximum_fusion), channel_id=1, source_target_pairs={{128,384},{129,385},{130,386},{131,387},{132,388},{133,389},{134,3... | collective-permute-start | bytes 98312 | tf_op jit(solution)/shard_map/ppermute | solution.py:40
  52.9 19.5 %collective-permute-start.4 = (bf16[4,552,128]{2,1,0:T(8,128)(2,1)S(1)}, bf16[4,552,128]{2,1,0:T(8,128)(2,1)S(1)}, u32[]{:S(2)}, u32[]{:S(2)}) collective-permute-start(bf16[4,552,128]{2,1,0:T(8,128)(2,1)S(1)} %get-tuple-element.24), channel_id=1, source_target_pairs={{0,2},{1,3},{2,4},{3,5},{4,6},{5,7},{6,8},{7,9},{8,10},{9,11},{10,... | collective-permute-start | bytes 1695752 | tf_op jit(solution)/shard_map/ppermute | solution.py:40
  58.9 13.5 %collective-permute-start.8 = (bf16[2,552,256]{2,1,0:T(8,128)(2,1)S(1)}, bf16[2,552,256]{2,1,0:T(8,128)(2,1)S(1)}, u32[]{:S(2)}, u32[]{:S(2)}) collective-permute-start(bf16[2,552,256]{2,1,0:T(8,128)(2,1)S(1)} %get-tuple-element.25.bot), channel_id=1, source_target_pairs={{0,32},{1,33},{2,34},{3,35},{4,36},{5,37},{6,38},{7,39},{8,40},{9,... | collective-permute-start | bytes 1695752 | tf_op jit(solution)/shard_map/ppermute | solution.py:40
  59.6 24.1 %collective-permute-start.11 = (bf16[4,552,256]{2,1,0:T(8,128)(2,1)S(1)}, bf16[4,552,256]{2,1,0:T(8,128)(2,1)S(1)}, u32[]{:S(2)}, u32[]{:S(2)}) collective-permute-start(bf16[4,552,256]{2,1,0:T(8,128)(2,1)S(1)} %get-tuple-element.30.refs_4_), channel_id=1, source_target_pairs={{0,1},{1,2},{2,3},{3,4},{4,5},{5,6},{6,7},{7,8},{8,9},{9,10},{10,1... | collective-permute-start | bytes 3391496 | tf_op jit(solution)/shard_map/ppermute | solution.py:40
  60.4 17.5 %collective-permute-start.10 = (bf16[4,552,128]{2,1,0:T(8,128)(2,1)S(1)}, bf16[4,552,128]{2,1,0:T(8,128)(2,1)S(1)}, u32[]{:S(2)}, u32[]{:S(2)}) collective-permute-start(bf16[4,552,128]{2,1,0:T(8,128)(2,1)S(1)} %get-tuple-element.29), channel_id=1, source_target_pairs={{0,31},{1,0},{2,1},{3,2},{4,3},{5,4},{6,5},{7,6},{8,7},{9,8},{10,9... | collective-permute-start | bytes 1695752 | tf_op jit(solution)/shard_map/ppermute | solution.py:40
  72.4 11.3 %collective-permute-start.9 = (bf16[4,552,128]{2,1,0:T(8,128)(2,1)S(1)}, bf16[4,552,128]{2,1,0:T(8,128)(2,1)S(1)}, u32[]{:S(2)}, u32[]{:S(2)}) collective-permute-start(bf16[4,552,128]{2,1,0:T(8,128)(2,1)S(1)} %collective-permute-done.4.refs_0_), channel_id=1, source_target_pairs={{128,384},{129,385},{130,386},{131,387},{132,388},{133,389},{134,3... | collective-permute-start | bytes 1695752 | tf_op jit(solution)/shard_map/ppermute | solution.py:40
  77.2 8.2 %collective-permute-start.12 = (bf16[2,552,256]{2,1,0:T(8,128)(2,1)S(1)}, bf16[2,552,256]{2,1,0:T(8,128)(2,1)S(1)}, u32[]{:S(2)}, u32[]{:S(2)}) collective-permute-start(bf16[2,552,256]{2,1,0:T(8,128)(2,1)S(1)} %get-tuple-element.27.refs_6_.top), channel_id=1, source_target_pairs={{32,0},{33,1},{34,2},{35,3},{36,4},{37,5},{38,6},{39,7},{40,8},{41... | collective-permute-start | bytes 1695752 | tf_op jit(solution)/shard_map/ppermute | solution.py:40
  88.2 21.1 %collective-permute-start.13 = (bf16[548,8,256]{2,1,0:T(8,128)(2,1)S(1)}, bf16[548,8,256]{2,1,0:T(8,128)(2,1)S(1)}, u32[]{:S(2)}, u32[]{:S(2)}) collective-permute-start(bf16[548,8,256]{2,1,0:T(8,128)(2,1)S(1)} %lat_rows.1), channel_id=1, source_target_pairs={{0,128},{1,129},{2,130},{3,131},{4,132},{5,133},{6,134},{7,135},{8... | collective-permute-start | bytes 6733832 | tf_op jit(solution)/shard_map/ppermute | solution.py:40

commit v2 on v1

--- a/solution.py
+++ b/solution.py
@@ -10,6 +10,7 @@
 BLK = 128
 AXES = ("tm", "lat", "lon")
 VMEM_LIMIT = 14 * 1024 * 1024
+LONG = pl.CostEstimate(flops=10**11, bytes_accessed=1000, transcendentals=0)
 SHORT = pl.CostEstimate(flops=1000, bytes_accessed=1000, transcendentals=0)
 VMEM = pl.BlockSpec(memory_space=pltpu.VMEM)
 
@@ -40,69 +41,99 @@
     return lax.ppermute(value, AXES, pairs)
 
 
-def split_kernel(x_ref, *refs, picked):
-    whole_ref, west_ref, east_ref, *wide = refs[-5:]
+def split_kernel(x_ref, *refs):
+    *outs, wide_west, wide_east = refs
     depth, rows, cols = x_ref.shape
-    padded = whole_ref.shape[1]
-    for g, (half_ref, buf) in enumerate(zip((west_ref, east_ref), wide)):
+    padded = outs[0].shape[1]
+    for g, buf in enumerate((wide_west, wide_east)):
         lanes = slice(g * BLK, (g + 1) * BLK)
         buf[: depth * rows] = x_ref[:, :, lanes].astype(jnp.float32).reshape(depth * rows, BLK)
         if padded > depth:
             buf[depth * rows :] = jnp.zeros(((padded - depth) * rows, BLK), jnp.float32)
-        for i, r in enumerate(picked):
-            slab = buf[pl.ds(r, padded, stride=rows), :].astype(jnp.bfloat16)
-            whole_ref[i, :, lanes] = slab
-            half_ref[i] = slab
-
-
-def split_rows(x, picked, padded, after=()):
-    depth, rows, cols = x.shape
-    n = len(picked)
-    half = jax.ShapeDtypeStruct((n, padded, cols // 2), x.dtype)
-    return pl.pallas_call(
-        functools.partial(split_kernel, picked=picked),
-        out_shape=(jax.ShapeDtypeStruct((n, padded, cols), x.dtype), half, half),
-        in_specs=[VMEM] + [pl.BlockSpec(memory_space=pl.ANY)] * len(after),
-        out_specs=(VMEM, VMEM, VMEM),
+        for picked, whole_ref, east_ref in zip(row_sets(rows), outs[:2], outs[2:]):
+            for i, r in enumerate(picked):
+                slab = buf[pl.ds(r, padded, stride=rows), :].astype(jnp.bfloat16)
+                whole_ref[i, :, lanes] = slab
+                if g == 1:
+                    east_ref[i] = slab
+
+
+def row_sets(rows):
+    return (0, 1, rows - 2, rows - 1), tuple(range(2, rows - 2))
+
+
+def split_rows(x, padded):
+    _, rows, cols = x.shape
+    edge, inner = row_sets(rows)
+    shapes = [(len(picked), padded, w) for w in (cols, cols // 2) for picked in (edge, inner)]
+    return pl.pallas_call(
+        split_kernel,
+        out_shape=[jax.ShapeDtypeStruct(shape, x.dtype) for shape in shapes],
+        in_specs=[VMEM],
+        out_specs=[VMEM] * 4,
         scratch_shapes=[pltpu.VMEM((padded * rows, BLK), jnp.float32)] * 2,
         compiler_params=params(),
         cost_estimate=SHORT,
         name="split_rows",
-    )(x, *after)
+    )(x)
 
 
 def choose_kernel(lent_flag, lent_ref, own_ref, own_east_ref, *refs):
     whole_ref, west_ref, east_ref = refs[-3:]
     half = west_ref.shape[2]
     east_ref[...] = own_east_ref[...]
-
-    def put(ref):
-        for r in range(whole_ref.shape[0]):
-            slab = ref[r]
-            whole_ref[r] = slab
-            west_ref[r] = slab[:, :half]
-
-    @pl.when(lent_flag[0] == 1)
-    def _():
-        put(lent_ref)
-
-    @pl.when(lent_flag[0] == 0)
-    def _():
-        put(own_ref)
+    for flag, ref in enumerate((own_ref, lent_ref)):
+
+        @pl.when(lent_flag[0] == flag)
+        def _():
+            whole_ref[...] = ref[...]
+            west_ref[...] = ref[:, :, :half]
 
 
 def choose(flag, lent, own, own_east, after):
+    count, depth, cols = own.shape
     half = jax.ShapeDtypeStruct(own_east.shape, own.dtype)
+
+    def block(width, index):
+        return pl.BlockSpec((1, depth, width), index)
+
+    def each(i, flag_ref):
+        return (i, 0, 0)
+
     return pl.pallas_call(
         choose_kernel,
+        grid_spec=pltpu.PrefetchScalarGridSpec(
+            num_scalar_prefetch=1,
+            grid=(count,),
+            in_specs=[
+                block(cols, lambda i, flag_ref: (i * flag_ref[0], 0, 0)),
+                block(cols, lambda i, flag_ref: (i * (1 - flag_ref[0]), 0, 0)),
+                block(cols // 2, each),
+            ]
+            + [pl.BlockSpec(memory_space=pl.ANY)] * len(after),
+            out_specs=[block(cols, each), block(cols // 2, each), block(cols // 2, each)],
+        ),
         out_shape=(jax.ShapeDtypeStruct(own.shape, own.dtype), half, half),
-        in_specs=[pl.BlockSpec(memory_space=pltpu.SMEM), VMEM, VMEM, VMEM]
-        + [pl.BlockSpec(memory_space=pl.ANY)] * len(after),
-        out_specs=(VMEM, VMEM, VMEM),
         compiler_params=params(),
         cost_estimate=SHORT,
         name="choose",
     )(flag, lent, own, own_east, *after)
+
+
+def token_kernel(*refs):
+    refs[-1][...] = jnp.zeros_like(refs[-1])
+
+
+def token(*after):
+    return pl.pallas_call(
+        token_kernel,
+        out_shape=jax.ShapeDtypeStruct((8, BLK), jnp.float32),
+        in_specs=[pl.BlockSpec(memory_space=pl.ANY)] * len(after),
+        out_specs=VMEM,
+        compiler_params=params(),
+        cost_estimate=LONG,
+        name="token",
+    )(*after)
 
 
 def matrix_kernel(geo_ref, m_ref):
@@ -256,12 +287,10 @@
     def neighbours(own, west_half):
         return move(own, along_lon(1), active), move(west_half, along_lon(-1), active)
 
-    edge, inner = (0, 1, rows - 2, rows - 1), tuple(range(2, rows - 2))
-    raw, _, east = split_rows(flat, edge, padded)
+    raw, raw_in, east, east_in = split_rows(flat, padded)
     far = move(east, along_lon(2), (0, 1, 2))
     own, west_half, _ = choose(flag, move(raw, lend, (1,)), raw, east, ())
     west, near = neighbours(own, west_half)
-    raw_in, _, east_in = split_rows(flat, inner, padded, (own,))
     lent_in = move(raw_in, lend, (1,))
     own_in, west_half_in, east_in = choose(flag, lent_in, raw_in, east_in, (near, geo))
     far_in = move(east_in, along_lon(2), (0, 1, 2))
@@ -271,7 +300,7 @@
     top, bot = lon_rows(flag, far, far_lent, near, west, own, m, ((0, 0), (2, rows - 2)), 2)
     above = move(bot, lambda t, b, j: (t, b + 1, j) if b + 1 < bands else None, active)
     below = move(top, lambda t, b, j: (t, b - 1, j) if b > 0 else None, active)
-    behind, above = lax.optimization_barrier((far_in, above))
+    behind, top = lax.optimization_barrier((far_in, top))
     far_lent_in = move(behind, lend, (1,))
     (mid,) = lon_rows(flag, far_in, far_lent_in, near_in, west_in, own_in, m, ((0, 2),), rows - 4, (top,))
     end = lat_rows(above, top, mid, bot, below, geo, depth)

time: 112 us -> 104 us (0.929)
  the two profiles are of different devices: /device:TPU:211 before, /device:TPU:43 now
where the time goes in v2:
time: 104 us; the launch traced here: 103 us
  waiting for transfers between devices  50.9 us (49%)
  starting transfers between devices  31.8 us (31%)
  Pallas kernels  15.8 us (15%)
  other arithmetic  2.26 us (2%)
  local copies, waits for them, and re-layouts  1.74 us (2%)
    ppermute x14, waiting for transfers between devices, move(): return lax.ppermute(value, AXES, pairs)  50.9 us
    ppermute x14, starting transfers between devices, move(): return lax.ppermute(value, AXES, pairs)  31.8 us
    pallas_call x2, Pallas kernels, choose(): pl.pallas_call(choose_kernel, grid_spec=pltpu.PrefetchScalarGridSpec(num_...  5.5 us
    pallas_call x2, Pallas kernels, lon_rows(): pl.pallas_call(functools.partial(lon_kernel, per_step=len(firsts)), grid=...  2.96 us
    pallas_call x1, Pallas kernels, lat_rows(): pl.pallas_call(lat_kernel, out_shape=jax.ShapeDtypeStruct((depth, rows, c...  2.81 us
    pallas_call x1, Pallas kernels, split_rows(): pl.pallas_call(split_kernel, out_shape=[jax.ShapeDtypeStruct(shape, x.dty...  2.37 us
    pallas_call x1, Pallas kernels, matrices(): pl.pallas_call(matrix_kernel, grid=(rows,), out_shape=jax.ShapeDtypeStruc...  2.14 us
    convert_element_type x1, other arithmetic, body(): (flat.astype(jnp.float32) - previous.astype(jnp.float32)).astype(jnp.bflo...  2.08 us
  transfers between devices with their start and end apart: 14, of which 6 were waited for; matrix products, arithmetic and copies ran while one was open for 0% of the time, Pallas kernels for 10%

profile of v2, /device:TPU:43, one launch (start us, length us, event | category | flops | bytes accessed | tf_op | source)
XLA Modules:
  0.0 103.5 jit_solution(12462654165603368199)
XLA Ops:
  0.0 1.6 %copy-done = bf16[1,4,137,8,256]{4,3,2,1,0:T(8,128)(2,1)S(1)} copy-done((bf16[1,4,137,8,256]{4,3,2,1,0:T(8,128)(2,1)S(1)}, bf16[1,4,137,8,256]{4,3,2,1,0:T(8,128)(2,1)}, u32[]{:S(2)}) %copy-start) | copy-done | bytes 2244632
  1.7 2.4 %split_rows.1 = (bf16[4,552,256]{2,1,0:T(8,128)(2,1)S(1)}, bf16[4,552,256]{2,1,0:T(8,128)(2,1)}, bf16[4,552,128]{2,1,0:T(8,128)(2,1)}, bf16[4,552,128]{2,1,0:T(8,128)(2,1)S(1)}) custom-call(bf16[548,8,256]{2,1,0:T(8,128)(2,1)S(1)} %bitcast.53), custom_call_target="tpu_custom_call" | custom-call | flops 1000 | bytes 1000 | tf_op jit(solution)/shard_map/split_rows/pallas_call | solution.py:69
  4.0 1.3 %collective-permute-start.2 = (bf16[4,552,256]{2,1,0:T(8,128)(2,1)S(1)}, bf16[4,552,256]{2,1,0:T(8,128)(2,1)S(1)}, u32[]{:S(2)}, u32[]{:S(2)}) collective-permute-start(bf16[4,552,256]{2,1,0:T(8,128)(2,1)S(1)} %get-tuple-element.19.own_ref), channel_id=1, source_target_pairs={{128,384},{129,385},{130,386},{131,387},{132,388},{133,389},{134,3... | collective-permute-start | bytes 3391496 | tf_op jit(solution)/shard_map/ppermute | solution.py:41
  5.3 1.3 %collective-permute-start.7 = (bf16[4,552,256]{2,1,0:T(8,128)(2,1)}, bf16[4,552,256]{2,1,0:T(8,128)(2,1)}, u32[]{:S(2)}, u32[]{:S(2)}) collective-permute-start(bf16[4,552,256]{2,1,0:T(8,128)(2,1)} %get-tuple-element.23.own_ref), channel_id=1, source_target_pairs={{128,384},{129,385},{130,386},{131,387},{132,388},{133,389},{134,3... | collective-permute-start | bytes 3391496 | tf_op jit(solution)/shard_map/ppermute | solution.py:41
  6.6 0.7 collective-permute-start
  8.1 0.1 broadcast_bitcast_fusion
  8.1 12.6 %collective-permute-done.2.lent_ref = bf16[4,552,256]{2,1,0:T(8,128)(2,1)S(1)} collective-permute-done((bf16[4,552,256]{2,1,0:T(8,128)(2,1)S(1)}, bf16[4,552,256]{2,1,0:T(8,128)(2,1)S(1)}, u32[]{:S(2)}, u32[]{:S(2)}) %collective-permute-start.2) | collective-permute-done | bytes 1130528 | tf_op jit(solution)/shard_map/ppermute | solution.py:41
  20.7 3.2 %choose.2 = (bf16[4,552,256]{2,1,0:T(8,128)(2,1)S(1)}, bf16[4,552,128]{2,1,0:T(8,128)(2,1)S(1)}, bf16[4,552,128]{2,1,0:T(8,128)(2,1)}) custom-call(s32[1]{0:T(128)} %bitcast.1.lent_flag, bf16[4,552,256]{2,1,0:T(8,128)(2,1)S(1)} %collective-permute-done.2.lent_ref, bf16[4,552,256]{2,1,0:T(8,128)(2,1)S(1)} %get-tuple-element.19.own_ref, ...), custom_call_target="tpu_custom_call" | custom-call | flops 1000 | bytes 1000 | tf_op jit(solution)/shard_map/choose/pallas_call | solution.py:103
  24.0 3.1 %collective-permute-start.4 = (bf16[4,552,256]{2,1,0:T(8,128)(2,1)S(1)}, bf16[4,552,256]{2,1,0:T(8,128)(2,1)S(1)}, u32[]{:S(2)}, u32[]{:S(2)}) collective-permute-start(bf16[4,552,256]{2,1,0:T(8,128)(2,1)S(1)} %get-tuple-element.21.refs_4_.refs_10_), channel_id=1, source_target_pairs={{0,1},{1,2},{2,3},{3,4},{4,5},{5,6},{6,7},{7,8},{8,9},{9,10},{10,1... | collective-permute-start | bytes 3391496 | tf_op jit(solution)/shard_map/ppermute | solution.py:41
  27.1 2.2 %collective-permute-start.3 = (bf16[4,552,128]{2,1,0:T(8,128)(2,1)S(1)}, bf16[4,552,128]{2,1,0:T(8,128)(2,1)S(1)}, u32[]{:S(2)}, u32[]{:S(2)}) collective-permute-start(bf16[4,552,128]{2,1,0:T(8,128)(2,1)S(1)} %get-tuple-element.20), channel_id=1, source_target_pairs={{0,31},{1,0},{2,1},{3,2},{4,3},{5,4},{6,5},{7,6},{8,7},{9,8},{10,9... | collective-permute-start | bytes 1695752 | tf_op jit(solution)/shard_map/ppermute | solution.py:41
  29.3 0.1 fusion.8
  29.5 1.3 %collective-permute-start.5 = (f32[4,8,256]{2,1,0:T(8,128)S(1)}, f32[4,8,256]{2,1,0:T(8,128)S(1)}, u32[]{:S(2)}, u32[]{:S(2)}) collective-permute-start(f32[4,8,256]{2,1,0:T(8,128)S(1)} %pad_maximum_fusion), channel_id=1, source_target_pairs={{128,384},{129,385},{130,386},{131,387},{132,388},{133,389},{134,3... | collective-permute-start | bytes 98312 | tf_op jit(solution)/shard_map/ppermute | solution.py:41
  30.8 3.7 %collective-permute-done.5 = f32[4,8,256]{2,1,0:T(8,128)S(1)} collective-permute-done((f32[4,8,256]{2,1,0:T(8,128)S(1)}, f32[4,8,256]{2,1,0:T(8,128)S(1)}, u32[]{:S(2)}, u32[]{:S(2)}) %collective-permute-start.5) | collective-permute-done | bytes 32800 | tf_op jit(solution)/shard_map/ppermute | solution.py:41
  34.4 1.3 %collective-permute-start.1 = (bf16[4,552,128]{2,1,0:T(8,128)(2,1)S(1)}, bf16[4,552,128]{2,1,0:T(8,128)(2,1)S(1)}, u32[]{:S(2)}, u32[]{:S(2)}) collective-permute-start(bf16[4,552,128]{2,1,0:T(8,128)(2,1)S(1)} %collective-permute-done.refs_0_.refs_6_), channel_id=1, source_target_pairs={{128,384},{129,385},{130,386},{131,387},{132,388},{133,389},{134,3... | collective-permute-start | bytes 1695752 | tf_op jit(solution)/shard_map/ppermute | solution.py:41
  35.7 3.1 %collective-permute-done.3.refs_2_.refs_8_.refs_0_ = bf16[4,552,128]{2,1,0:T(8,128)(2,1)S(1)} collective-permute-done((bf16[4,552,128]{2,1,0:T(8,128)(2,1)S(1)}, bf16[4,552,128]{2,1,0:T(8,128)(2,1)S(1)}, u32[]{:S(2)}, u32[]{:S(2)}) %collective-permute-start.3) | collective-permute-done | bytes 565280 | tf_op jit(solution)/shard_map/ppermute | solution.py:41
  38.9 2.3 %choose.3 = (bf16[4,552,256]{2,1,0:T(8,128)(2,1)S(1)}, bf16[4,552,128]{2,1,0:T(8,128)(2,1)S(1)}, bf16[4,552,128]{2,1,0:T(8,128)(2,1)S(1)}) custom-call(s32[1]{0:T(128)} %bitcast.1.lent_flag, bf16[4,552,256]{2,1,0:T(8,128)(2,1)} %collective-permute-done.7.lent_ref, bf16[4,552,256]{2,1,0:T(8,128)(2,1)} %get-tuple-element.23.own_ref, ...), custom_call_target="tpu_custom_call" | custom-call | flops 1000 | bytes 1000 | tf_op jit(solution)/shard_map/choose/pallas_call | solution.py:103
  41.1 0.7 collective-permute-start.8
  41.8 2.2 %collective-permute-start.11 = (bf16[4,552,256]{2,1,0:T(8,128)(2,1)S(1)}, bf16[4,552,256]{2,1,0:T(8,128)(2,1)S(1)}, u32[]{:S(2)}, u32[]{:S(2)}) collective-permute-start(bf16[4,552,256]{2,1,0:T(8,128)(2,1)S(1)} %get-tuple-element.30.refs_4_), channel_id=1, source_target_pairs={{0,1},{1,2},{2,3},{3,4},{4,5},{5,6},{6,7},{7,8},{8,9},{9,10},{10,1... | collective-permute-start | bytes 3391496 | tf_op jit(solution)/shard_map/ppermute | solution.py:41
  44.0 2.1 %matrices.1.refs_5_.refs_11_ = bf16[8,768,256]{2,1,0:T(8,128)(2,1)S(1)} custom-call(f32[4,8,256]{2,1,0:T(8,128)S(1)} %broadcast_select_fusion.geo_ref.refs_1_), custom_call_target="tpu_custom_call" | custom-call | flops 1000 | bytes 1000 | tf_op jit(solution)/shard_map/matrices/pallas_call | solution.py:155
  46.2 8.3 %collective-permute-start.10 = (bf16[4,552,128]{2,1,0:T(8,128)(2,1)S(1)}, bf16[4,552,128]{2,1,0:T(8,128)(2,1)S(1)}, u32[]{:S(2)}, u32[]{:S(2)}) collective-permute-start(bf16[4,552,128]{2,1,0:T(8,128)(2,1)S(1)} %get-tuple-element.29), channel_id=1, source_target_pairs={{0,31},{1,0},{2,1},{3,2},{4,3},{5,4},{6,5},{7,6},{8,7},{9,8},{10,9... | collective-permute-start | bytes 1695752 | tf_op jit(solution)/shard_map/ppermute | solution.py:41
  54.5 1.3 %lon_rows.2 = (bf16[2,552,256]{2,1,0:T(8,128)(2,1)S(1)}, bf16[2,552,256]{2,1,0:T(8,128)(2,1)S(1)}) custom-call(s32[1]{0:T(128)} %bitcast.1.lent_flag, bf16[4,552,128]{2,1,0:T(8,128)(2,1)S(1)} %collective-permute-done.refs_0_.refs_6_, bf16[4,552,128]{2,1,0:T(8,128)(2,1)S(1)} %collective-permute-done.1.refs_1_.refs_7_, ...), custom_call_target="tpu_custom_call" | custom-call | flops 1000 | bytes 1000 | tf_op jit(solution)/shard_map/lon_rows/pallas_call | solution.py:196
  55.9 1.3 %collective-permute-start.9 = (bf16[4,552,128]{2,1,0:T(8,128)(2,1)S(1)}, bf16[4,552,128]{2,1,0:T(8,128)(2,1)S(1)}, u32[]{:S(2)}, u32[]{:S(2)}) collective-permute-start(bf16[4,552,128]{2,1,0:T(8,128)(2,1)S(1)} %collective-permute-done.8.refs_0_), channel_id=1, source_target_pairs={{128,384},{129,385},{130,386},{131,387},{132,388},{133,389},{134,3... | collective-permute-start | bytes 1695752 | tf_op jit(solution)/shard_map/ppermute | solution.py:41
  57.2 2.9 %collective-permute-start.12 = (bf16[2,552,256]{2,1,0:T(8,128)(2,1)S(1)}, bf16[2,552,256]{2,1,0:T(8,128)(2,1)S(1)}, u32[]{:S(2)}, u32[]{:S(2)}) collective-permute-start(bf16[2,552,256]{2,1,0:T(8,128)(2,1)S(1)} %get-tuple-element.27.refs_6_.top), channel_id=1, source_target_pairs={{32,0},{33,1},{34,2},{35,3},{36,4},{37,5},{38,6},{39,7},{40,8},{41... | collective-permute-start | bytes 1695752 | tf_op jit(solution)/shard_map/ppermute | solution.py:41
  60.0 3.4 %collective-permute-start.6 = (bf16[2,552,256]{2,1,0:T(8,128)(2,1)S(1)}, bf16[2,552,256]{2,1,0:T(8,128)(2,1)S(1)}, u32[]{:S(2)}, u32[]{:S(2)}) collective-permute-start(bf16[2,552,256]{2,1,0:T(8,128)(2,1)S(1)} %get-tuple-element.22.bot), channel_id=1, source_target_pairs={{0,32},{1,33},{2,34},{3,35},{4,36},{5,37},{6,38},{7,39},{8,40},{9,... | collective-permute-start | bytes 1695752 | tf_op jit(solution)/shard_map/ppermute | solution.py:41
  63.4 2.4 %collective-permute-done.10.refs_2_ = bf16[4,552,128]{2,1,0:T(8,128)(2,1)S(1)} collective-permute-done((bf16[4,552,128]{2,1,0:T(8,128)(2,1)S(1)}, bf16[4,552,128]{2,1,0:T(8,128)(2,1)S(1)}, u32[]{:S(2)}, u32[]{:S(2)}) %collective-permute-start.10) | collective-permute-done | bytes 565280 | tf_op jit(solution)/shard_map/ppermute | solution.py:41
  65.8 24.8 %collective-permute-done.9.refs_1_ = bf16[4,552,128]{2,1,0:T(8,128)(2,1)S(1)} collective-permute-done((bf16[4,552,128]{2,1,0:T(8,128)(2,1)S(1)}, bf16[4,552,128]{2,1,0:T(8,128)(2,1)S(1)}, u32[]{:S(2)}, u32[]{:S(2)}) %collective-permute-start.9) | collective-permute-done | bytes 565280 | tf_op jit(solution)/shard_map/ppermute | solution.py:41
  90.6 1.7 %lon_rows.3.mid = bf16[4,552,256]{2,1,0:T(8,128)(2,1)S(1)} custom-call(s32[1]{0:T(128)} %bitcast.1.lent_flag, bf16[4,552,128]{2,1,0:T(8,128)(2,1)S(1)} %collective-permute-done.8.refs_0_, bf16[4,552,128]{2,1,0:T(8,128)(2,1)S(1)} %collective-permute-done.9.refs_1_, bf16[4,552,128]{2,1,0:T(8,128)(2,1)S(1)} %collective-permute-done.10.refs_2_, ...), custom_call_target="tpu_custom_call" | custom-call | flops 1000 | bytes 1000 | tf_op jit(solution)/shard_map/lon_rows/pallas_call | solution.py:196
  92.3 0.0 copy-start.1
  92.3 2.8 %lat_rows.1 = bf16[548,8,256]{2,1,0:T(8,128)(2,1)S(1)} custom-call(bf16[2,552,256]{2,1,0:T(8,128)(2,1)S(1)} %collective-permute-done.6.above, bf16[2,552,256]{2,1,0:T(8,128)(2,1)S(1)} %get-tuple-element.27.refs_6_.top, bf16[4,552,256]{2,1,0:T(8,128)(2,1)S(1)} %lon_rows.3.mid, bf16[2,552,256]{2,1,0:T(8,128)(2,1)S(1)} %get-tuple-element.22.bot, ...), custom_call_target="tpu_custom_call" | custom-call | flops 1000 | bytes 1000 | tf_op jit(solution)/shard_map/lat_rows/pallas_call | solution.py:237
  95.1 1.9 %collective-permute-start.13 = (bf16[548,8,256]{2,1,0:T(8,128)(2,1)S(1)}, bf16[548,8,256]{2,1,0:T(8,128)(2,1)S(1)}, u32[]{:S(2)}, u32[]{:S(2)}) collective-permute-start(bf16[548,8,256]{2,1,0:T(8,128)(2,1)S(1)} %lat_rows.1), channel_id=1, source_target_pairs={{0,128},{1,129},{2,130},{3,131},{4,132},{5,133},{6,134},{7,135},{8... | collective-permute-start | bytes 6733832 | tf_op jit(solution)/shard_map/ppermute | solution.py:41
  97.0 4.3 %collective-permute-done.13 = bf16[548,8,256]{2,1,0:T(8,128)(2,1)S(1)} collective-permute-done((bf16[548,8,256]{2,1,0:T(8,128)(2,1)S(1)}, bf16[548,8,256]{2,1,0:T(8,128)(2,1)S(1)}, u32[]{:S(2)}, u32[]{:S(2)}) %collective-permute-start.13) | collective-permute-done | bytes 2244640 | tf_op jit(solution)/shard_map/ppermute | solution.py:41
  101.4 2.1 %subtract_convert_fusion = bf16[548,8,256]{2,1,0:T(8,128)(2,1)} fusion(bf16[548,8,256]{2,1,0:T(8,128)(2,1)S(1)} %collective-permute-done.13, bf16[1,4,137,8,256]{4,3,2,1,0:T(8,128)(2,1)S(1)} %copy-done.1), kind=kLoop, calls=%fused_computation | loop fusion | flops 4489216 | bytes 6733824 | tf_op jit(solution)/shard_map/convert_element_type | solution.py:308
  (26 shorter events, 0.1 us)
Async XLA Ops:
  0.0 1.6 %copy-start = (bf16[1,4,137,8,256]{4,3,2,1,0:T(8,128)(2,1)S(1)}, bf16[1,4,137,8,256]{4,3,2,1,0:T(8,128)(2,1)}, u32[]{:S(2)}) copy-start(bf16[1,4,137,8,256]{4,3,2,1,0:T(8,128)(2,1)} %param.8) | copy-start | bytes 6733828
  1.6 6.4 %copy-start.6 = (s32[1,8,256]{2,1,0:T(8,128)S(1)}, s32[1,8,256]{2,1,0:T(8,128)}, u32[]{:S(2)}) copy-start(s32[1,8,256]{2,1,0:T(8,128)} %param.14) | copy-start | bytes 24580
  1.6 6.4 %copy-start.7 = (s32[1,8,2,6]{1,2,3,0:T(2,128)S(1)}, s32[1,8,2,6]{1,2,3,0:T(2,128)}, u32[]{:S(2)}) copy-start(s32[1,8,2,6]{1,2,3,0:T(2,128)} %param.10) | copy-start | bytes 1156
  1.6 27.6 %copy-start.4 = (s32[1,8,256]{2,1,0:T(8,128)S(1)}, s32[1,8,256]{2,1,0:T(8,128)}, u32[]{:S(2)}) copy-start(s32[1,8,256]{2,1,0:T(8,128)} %param.12) | copy-start | bytes 24580
  1.6 27.6 %copy-start.5 = (s32[1,8,256]{2,1,0:T(8,128)S(1)}, s32[1,8,256]{2,1,0:T(8,128)}, u32[]{:S(2)}) copy-start(s32[1,8,256]{2,1,0:T(8,128)} %param.11) | copy-start | bytes 24580
  1.6 27.8 %copy-start.2 = (f32[1,8,256]{2,1,0:T(8,128)S(1)}, f32[1,8,256]{2,1,0:T(8,128)}, u32[]{:S(2)}) copy-start(f32[1,8,256]{2,1,0:T(8,128)} %param.15) | copy-start | bytes 24580
  1.7 27.8 %copy-start.3 = (f32[1,8,256]{2,1,0:T(8,128)S(1)}, f32[1,8,256]{2,1,0:T(8,128)}, u32[]{:S(2)}) copy-start(f32[1,8,256]{2,1,0:T(8,128)} %param.13) | copy-start | bytes 24580
  4.0 16.7 %collective-permute-start.2 = (bf16[4,552,256]{2,1,0:T(8,128)(2,1)S(1)}, bf16[4,552,256]{2,1,0:T(8,128)(2,1)S(1)}, u32[]{:S(2)}, u32[]{:S(2)}) collective-permute-start(bf16[4,552,256]{2,1,0:T(8,128)(2,1)S(1)} %get-tuple-element.19.own_ref), channel_id=1, source_target_pairs={{128,384},{129,385},{130,386},{131,387},{132,388},{133,389},{134,3... | collective-permute-start | bytes 3391496 | tf_op jit(solution)/shard_map/ppermute | solution.py:41
  5.3 30.4 %collective-permute-start.7 = (bf16[4,552,256]{2,1,0:T(8,128)(2,1)}, bf16[4,552,256]{2,1,0:T(8,128)(2,1)}, u32[]{:S(2)}, u32[]{:S(2)}) collective-permute-start(bf16[4,552,256]{2,1,0:T(8,128)(2,1)} %get-tuple-element.23.own_ref), channel_id=1, source_target_pairs={{128,384},{129,385},{130,386},{131,387},{132,388},{133,389},{134,3... | collective-permute-start | bytes 3391496 | tf_op jit(solution)/shard_map/ppermute | solution.py:41
  6.6 27.8 %collective-permute-start = (bf16[4,552,128]{2,1,0:T(8,128)(2,1)}, bf16[4,552,128]{2,1,0:T(8,128)(2,1)S(1)}, u32[]{:S(2)}, u32[]{:S(2)}) collective-permute-start(bf16[4,552,128]{2,1,0:T(8,128)(2,1)} %get-tuple-element.18.own_east_ref), channel_id=1, source_target_pairs={{0,2},{1,3},{2,4},{3,5},{4,6},{5,7},{6,8},{7,9},{8,10},{9,11},{10,... | collective-permute-start | bytes 1695752 | tf_op jit(solution)/shard_map/ppermute | solution.py:41
  24.0 30.6 %collective-permute-start.4 = (bf16[4,552,256]{2,1,0:T(8,128)(2,1)S(1)}, bf16[4,552,256]{2,1,0:T(8,128)(2,1)S(1)}, u32[]{:S(2)}, u32[]{:S(2)}) collective-permute-start(bf16[4,552,256]{2,1,0:T(8,128)(2,1)S(1)} %get-tuple-element.21.refs_4_.refs_10_), channel_id=1, source_target_pairs={{0,1},{1,2},{2,3},{3,4},{4,5},{5,6},{6,7},{7,8},{8,9},{9,10},{10,1... | collective-permute-start | bytes 3391496 | tf_op jit(solution)/shard_map/ppermute | solution.py:41
  27.1 11.8 %collective-permute-start.3 = (bf16[4,552,128]{2,1,0:T(8,128)(2,1)S(1)}, bf16[4,552,128]{2,1,0:T(8,128)(2,1)S(1)}, u32[]{:S(2)}, u32[]{:S(2)}) collective-permute-start(bf16[4,552,128]{2,1,0:T(8,128)(2,1)S(1)} %get-tuple-element.20), channel_id=1, source_target_pairs={{0,31},{1,0},{2,1},{3,2},{4,3},{5,4},{6,5},{7,6},{8,7},{9,8},{10,9... | collective-permute-start | bytes 1695752 | tf_op jit(solution)/shard_map/ppermute | solution.py:41
  29.5 5.0 %collective-permute-start.5 = (f32[4,8,256]{2,1,0:T(8,128)S(1)}, f32[4,8,256]{2,1,0:T(8,128)S(1)}, u32[]{:S(2)}, u32[]{:S(2)}) collective-permute-start(f32[4,8,256]{2,1,0:T(8,128)S(1)} %pad_maximum_fusion), channel_id=1, source_target_pairs={{128,384},{129,385},{130,386},{131,387},{132,388},{133,389},{134,3... | collective-permute-start | bytes 98312 | tf_op jit(solution)/shard_map/ppermute | solution.py:41
  34.4 20.1 %collective-permute-start.1 = (bf16[4,552,128]{2,1,0:T(8,128)(2,1)S(1)}, bf16[4,552,128]{2,1,0:T(8,128)(2,1)S(1)}, u32[]{:S(2)}, u32[]{:S(2)}) collective-permute-start(bf16[4,552,128]{2,1,0:T(8,128)(2,1)S(1)} %collective-permute-done.refs_0_.refs_6_), channel_id=1, source_target_pairs={{128,384},{129,385},{130,386},{131,387},{132,388},{133,389},{134,3... | collective-permute-start | bytes 1695752 | tf_op jit(solution)/shard_map/ppermute | solution.py:41
  41.1 14.8 %collective-permute-start.8 = (bf16[4,552,128]{2,1,0:T(8,128)(2,1)S(1)}, bf16[4,552,128]{2,1,0:T(8,128)(2,1)S(1)}, u32[]{:S(2)}, u32[]{:S(2)}) collective-permute-start(bf16[4,552,128]{2,1,0:T(8,128)(2,1)S(1)} %get-tuple-element.25), channel_id=1, source_target_pairs={{0,2},{1,3},{2,4},{3,5},{4,6},{5,7},{6,8},{7,9},{8,10},{9,11},{10,... | collective-permute-start | bytes 1695752 | tf_op jit(solution)/shard_map/ppermute | solution.py:41
  41.8 48.8 %collective-permute-start.11 = (bf16[4,552,256]{2,1,0:T(8,128)(2,1)S(1)}, bf16[4,552,256]{2,1,0:T(8,128)(2,1)S(1)}, u32[]{:S(2)}, u32[]{:S(2)}) collective-permute-start(bf16[4,552,256]{2,1,0:T(8,128)(2,1)S(1)} %get-tuple-element.30.refs_4_), channel_id=1, source_target_pairs={{0,1},{1,2},{2,3},{3,4},{4,5},{5,6},{6,7},{7,8},{8,9},{9,10},{10,1... | collective-permute-start | bytes 3391496 | tf_op jit(solution)/shard_map/ppermute | solution.py:41
  46.2 19.6 %collective-permute-start.10 = (bf16[4,552,128]{2,1,0:T(8,128)(2,1)S(1)}, bf16[4,552,128]{2,1,0:T(8,128)(2,1)S(1)}, u32[]{:S(2)}, u32[]{:S(2)}) collective-permute-start(bf16[4,552,128]{2,1,0:T(8,128)(2,1)S(1)} %get-tuple-element.29), channel_id=1, source_target_pairs={{0,31},{1,0},{2,1},{3,2},{4,3},{5,4},{6,5},{7,6},{8,7},{9,8},{10,9... | collective-permute-start | bytes 1695752 | tf_op jit(solution)/shard_map/ppermute | solution.py:41
  55.9 34.7 %collective-permute-start.9 = (bf16[4,552,128]{2,1,0:T(8,128)(2,1)S(1)}, bf16[4,552,128]{2,1,0:T(8,128)(2,1)S(1)}, u32[]{:S(2)}, u32[]{:S(2)}) collective-permute-start(bf16[4,552,128]{2,1,0:T(8,128)(2,1)S(1)} %collective-permute-done.8.refs_0_), channel_id=1, source_target_pairs={{128,384},{129,385},{130,386},{131,387},{132,388},{133,389},{134,3... | collective-permute-start | bytes 1695752 | tf_op jit(solution)/shard_map/ppermute | solution.py:41
  57.2 35.1 %collective-permute-start.12 = (bf16[2,552,256]{2,1,0:T(8,128)(2,1)S(1)}, bf16[2,552,256]{2,1,0:T(8,128)(2,1)S(1)}, u32[]{:S(2)}, u32[]{:S(2)}) collective-permute-start(bf16[2,552,256]{2,1,0:T(8,128)(2,1)S(1)} %get-tuple-element.27.refs_6_.top), channel_id=1, source_target_pairs={{32,0},{33,1},{34,2},{35,3},{36,4},{37,5},{38,6},{39,7},{40,8},{41... | collective-permute-start | bytes 1695752 | tf_op jit(solution)/shard_map/ppermute | solution.py:41
  60.0 32.2 %collective-permute-start.6 = (bf16[2,552,256]{2,1,0:T(8,128)(2,1)S(1)}, bf16[2,552,256]{2,1,0:T(8,128)(2,1)S(1)}, u32[]{:S(2)}, u32[]{:S(2)}) collective-permute-start(bf16[2,552,256]{2,1,0:T(8,128)(2,1)S(1)} %get-tuple-element.22.bot), channel_id=1, source_target_pairs={{0,32},{1,33},{2,34},{3,35},{4,36},{5,37},{6,38},{7,39},{8,40},{9,... | collective-permute-start | bytes 1695752 | tf_op jit(solution)/shard_map/ppermute | solution.py:41
  92.3 9.1 %copy-start.1 = (bf16[1,4,137,8,256]{4,3,2,1,0:T(8,128)(2,1)S(1)}, bf16[1,4,137,8,256]{4,3,2,1,0:T(8,128)(2,1)}, u32[]{:S(2)}) copy-start(bf16[1,4,137,8,256]{4,3,2,1,0:T(8,128)(2,1)} %param.8) | copy-start | bytes 6733828
  95.1 6.3 %collective-permute-start.13 = (bf16[548,8,256]{2,1,0:T(8,128)(2,1)S(1)}, bf16[548,8,256]{2,1,0:T(8,128)(2,1)S(1)}, u32[]{:S(2)}, u32[]{:S(2)}) collective-permute-start(bf16[548,8,256]{2,1,0:T(8,128)(2,1)S(1)} %lat_rows.1), channel_id=1, source_target_pairs={{0,128},{1,129},{2,130},{3,131},{4,132},{5,133},{6,134},{7,135},{8... | collective-permute-start | bytes 6733832 | tf_op jit(solution)/shard_map/ppermute | solution.py:41

commit v3 on v2

--- a/solution.py
+++ b/solution.py
@@ -300,7 +300,7 @@
     top, bot = lon_rows(flag, far, far_lent, near, west, own, m, ((0, 0), (2, rows - 2)), 2)
     above = move(bot, lambda t, b, j: (t, b + 1, j) if b + 1 < bands else None, active)
     below = move(top, lambda t, b, j: (t, b - 1, j) if b > 0 else None, active)
-    behind, top = lax.optimization_barrier((far_in, top))
+    behind = far_in
     far_lent_in = move(behind, lend, (1,))
     (mid,) = lon_rows(flag, far_in, far_lent_in, near_in, west_in, own_in, m, ((0, 2),), rows - 4, (top,))
     end = lat_rows(above, top, mid, bot, below, geo, depth)

time: 104 us -> 103 us (level)
  the two profiles are of different devices: /device:TPU:43 before, /device:TPU:49 now
where the time goes in v3:
time: 103 us; the launch traced here: 102 us
  waiting for transfers between devices  42.7 us (41%)
  starting transfers between devices  39.6 us (38%)
  Pallas kernels  14 us (14%)
  local copies, waits for them, and re-layouts  2.55 us (2%)
  other arithmetic  2.26 us (2%)
    ppermute x14, waiting for transfers between devices, move(): return lax.ppermute(value, AXES, pairs)  42.7 us
    ppermute x14, starting transfers between devices, move(): return lax.ppermute(value, AXES, pairs)  39.6 us
    pallas_call x2, Pallas kernels, choose(): pl.pallas_call(choose_kernel, grid_spec=pltpu.PrefetchScalarGridSpec(num_...  3.79 us
    pallas_call x2, Pallas kernels, lon_rows(): pl.pallas_call(functools.partial(lon_kernel, per_step=len(firsts)), grid=...  2.94 us
    pallas_call x1, Pallas kernels, lat_rows(): pl.pallas_call(lat_kernel, out_shape=jax.ShapeDtypeStruct((depth, rows, c...  2.81 us
    unnamed x20, local copies, waits for them, and re-layouts  2.47 us
    pallas_call x1, Pallas kernels, split_rows(): pl.pallas_call(split_kernel, out_shape=[jax.ShapeDtypeStruct(shape, x.dty...  2.36 us
    pallas_call x1, Pallas kernels, matrices(): pl.pallas_call(matrix_kernel, grid=(rows,), out_shape=jax.ShapeDtypeStruc...  2.14 us
  transfers between devices with their start and end apart: 14, of which 5 were waited for; matrix products, arithmetic and copies ran while one was open for 0% of the time, Pallas kernels for 9%

profile of v3, /device:TPU:49, one launch (start us, length us, event | category | flops | bytes accessed | tf_op | source)
XLA Modules:
  0.0 102.1 jit_solution(18383223230047504716)
XLA Ops:
  0.0 1.6 %copy-done = bf16[1,4,137,8,256]{4,3,2,1,0:T(8,128)(2,1)S(1)} copy-done((bf16[1,4,137,8,256]{4,3,2,1,0:T(8,128)(2,1)S(1)}, bf16[1,4,137,8,256]{4,3,2,1,0:T(8,128)(2,1)}, u32[]{:S(2)}) %copy-start) | copy-done | bytes 2244632
  1.7 2.4 %split_rows.1 = (bf16[4,552,256]{2,1,0:T(8,128)(2,1)S(1)}, bf16[4,552,256]{2,1,0:T(8,128)(2,1)}, bf16[4,552,128]{2,1,0:T(8,128)(2,1)S(1)}, bf16[4,552,128]{2,1,0:T(8,128)(2,1)S(1)}) custom-call(bf16[548,8,256]{2,1,0:T(8,128)(2,1)S(1)} %bitcast.53), custom_call_target="tpu_custom_call" | custom-call | flops 1000 | bytes 1000 | tf_op jit(solution)/shard_map/split_rows/pallas_call | solution.py:69
  4.0 0.8 copy-done.2
  4.8 2.4 %collective-permute-start.2 = (bf16[4,552,256]{2,1,0:T(8,128)(2,1)S(1)}, bf16[4,552,256]{2,1,0:T(8,128)(2,1)S(1)}, u32[]{:S(2)}, u32[]{:S(2)}) collective-permute-start(bf16[4,552,256]{2,1,0:T(8,128)(2,1)S(1)} %get-tuple-element.17.own_ref), channel_id=1, source_target_pairs={{128,384},{129,385},{130,386},{131,387},{132,388},{133,389},{134,3... | collective-permute-start | bytes 3391496 | tf_op jit(solution)/shard_map/ppermute | solution.py:41
  7.2 2.3 %collective-permute-start.7 = (bf16[4,552,256]{2,1,0:T(8,128)(2,1)}, bf16[4,552,256]{2,1,0:T(8,128)(2,1)}, u32[]{:S(2)}, u32[]{:S(2)}) collective-permute-start(bf16[4,552,256]{2,1,0:T(8,128)(2,1)} %get-tuple-element.22.own_ref), channel_id=1, source_target_pairs={{128,384},{129,385},{130,386},{131,387},{132,388},{133,389},{134,3... | collective-permute-start | bytes 3391496 | tf_op jit(solution)/shard_map/ppermute | solution.py:41
  9.5 4.6 %collective-permute-start = (bf16[4,552,128]{2,1,0:T(8,128)(2,1)S(1)}, bf16[4,552,128]{2,1,0:T(8,128)(2,1)S(1)}, u32[]{:S(2)}, u32[]{:S(2)}) collective-permute-start(bf16[4,552,128]{2,1,0:T(8,128)(2,1)S(1)} %get-tuple-element.16.own_east_ref), channel_id=1, source_target_pairs={{0,2},{1,3},{2,4},{3,5},{4,6},{5,7},{6,8},{7,9},{8,10},{9,11},{10,... | collective-permute-start | bytes 1695752 | tf_op jit(solution)/shard_map/ppermute | solution.py:41
  14.9 0.1 broadcast_bitcast_fusion
  15.0 4.8 %collective-permute-done.2.lent_ref = bf16[4,552,256]{2,1,0:T(8,128)(2,1)S(1)} collective-permute-done((bf16[4,552,256]{2,1,0:T(8,128)(2,1)S(1)}, bf16[4,552,256]{2,1,0:T(8,128)(2,1)S(1)}, u32[]{:S(2)}, u32[]{:S(2)}) %collective-permute-start.2) | collective-permute-done | bytes 1130528 | tf_op jit(solution)/shard_map/ppermute | solution.py:41
  19.7 1.5 %choose.2 = (bf16[4,552,256]{2,1,0:T(8,128)(2,1)S(1)}, bf16[4,552,128]{2,1,0:T(8,128)(2,1)S(1)}, bf16[4,552,128]{2,1,0:T(8,128)(2,1)}) custom-call(s32[1]{0:T(128)} %bitcast.1.lent_flag, bf16[4,552,256]{2,1,0:T(8,128)(2,1)S(1)} %collective-permute-done.2.lent_ref, bf16[4,552,256]{2,1,0:T(8,128)(2,1)S(1)} %get-tuple-element.17.own_ref, ...), custom_call_target="tpu_custom_call" | custom-call | flops 1000 | bytes 1000 | tf_op jit(solution)/shard_map/choose/pallas_call | solution.py:103
  21.2 0.7 collective-permute-start.4
  22.0 0.7 collective-permute-start.3
  22.7 0.1 fusion.8
  22.9 17.4 %collective-permute-start.5 = (f32[4,8,256]{2,1,0:T(8,128)S(1)}, f32[4,8,256]{2,1,0:T(8,128)S(1)}, u32[]{:S(2)}, u32[]{:S(2)}) collective-permute-start(f32[4,8,256]{2,1,0:T(8,128)S(1)} %pad_maximum_fusion), channel_id=1, source_target_pairs={{128,384},{129,385},{130,386},{131,387},{132,388},{133,389},{134,3... | collective-permute-start | bytes 98312 | tf_op jit(solution)/shard_map/ppermute | solution.py:41
  40.3 1.0 collective-permute-done.5
  41.4 2.3 %choose.3 = (bf16[4,552,256]{2,1,0:T(8,128)(2,1)S(1)}, bf16[4,552,128]{2,1,0:T(8,128)(2,1)S(1)}, bf16[4,552,128]{2,1,0:T(8,128)(2,1)S(1)}) custom-call(s32[1]{0:T(128)} %bitcast.1.lent_flag, bf16[4,552,256]{2,1,0:T(8,128)(2,1)} %collective-permute-done.7.lent_ref, bf16[4,552,256]{2,1,0:T(8,128)(2,1)} %get-tuple-element.22.own_ref, ...), custom_call_target="tpu_custom_call" | custom-call | flops 1000 | bytes 1000 | tf_op jit(solution)/shard_map/choose/pallas_call | solution.py:103
  43.7 1.9 %collective-permute-start.8 = (bf16[4,552,128]{2,1,0:T(8,128)(2,1)S(1)}, bf16[4,552,128]{2,1,0:T(8,128)(2,1)S(1)}, u32[]{:S(2)}, u32[]{:S(2)}) collective-permute-start(bf16[4,552,128]{2,1,0:T(8,128)(2,1)S(1)} %get-tuple-element.24), channel_id=1, source_target_pairs={{0,2},{1,3},{2,4},{3,5},{4,6},{5,7},{6,8},{7,9},{8,10},{9,11},{10,... | collective-permute-start | bytes 1695752 | tf_op jit(solution)/shard_map/ppermute | solution.py:41
  45.6 4.1 %collective-permute-start.1 = (bf16[4,552,128]{2,1,0:T(8,128)(2,1)S(1)}, bf16[4,552,128]{2,1,0:T(8,128)(2,1)S(1)}, u32[]{:S(2)}, u32[]{:S(2)}) collective-permute-start(bf16[4,552,128]{2,1,0:T(8,128)(2,1)S(1)} %collective-permute-done.refs_0_.refs_6_), channel_id=1, source_target_pairs={{128,384},{129,385},{130,386},{131,387},{132,388},{133,389},{134,3... | collective-permute-start | bytes 1695752 | tf_op jit(solution)/shard_map/ppermute | solution.py:41
  49.7 0.7 collective-permute-start.11
  50.4 2.1 %matrices.1.refs_5_.refs_11_ = bf16[8,768,256]{2,1,0:T(8,128)(2,1)S(1)} custom-call(f32[4,8,256]{2,1,0:T(8,128)S(1)} %broadcast_select_fusion.geo_ref.refs_1_), custom_call_target="tpu_custom_call" | custom-call | flops 1000 | bytes 1000 | tf_op jit(solution)/shard_map/matrices/pallas_call | solution.py:155
  52.6 0.7 collective-permute-start.10
  53.3 9.8 %collective-permute-done.8.refs_0_ = bf16[4,552,128]{2,1,0:T(8,128)(2,1)S(1)} collective-permute-done((bf16[4,552,128]{2,1,0:T(8,128)(2,1)S(1)}, bf16[4,552,128]{2,1,0:T(8,128)(2,1)S(1)}, u32[]{:S(2)}, u32[]{:S(2)}) %collective-permute-start.8) | collective-permute-done | bytes 565280 | tf_op jit(solution)/shard_map/ppermute | solution.py:41
  63.1 1.3 %collective-permute-start.9 = (bf16[4,552,128]{2,1,0:T(8,128)(2,1)S(1)}, bf16[4,552,128]{2,1,0:T(8,128)(2,1)S(1)}, u32[]{:S(2)}, u32[]{:S(2)}) collective-permute-start(bf16[4,552,128]{2,1,0:T(8,128)(2,1)S(1)} %collective-permute-done.8.refs_0_), channel_id=1, source_target_pairs={{128,384},{129,385},{130,386},{131,387},{132,388},{133,389},{134,3... | collective-permute-start | bytes 1695752 | tf_op jit(solution)/shard_map/ppermute | solution.py:41
  64.4 1.3 %lon_rows.2 = (bf16[2,552,256]{2,1,0:T(8,128)(2,1)S(1)}, bf16[2,552,256]{2,1,0:T(8,128)(2,1)S(1)}) custom-call(s32[1]{0:T(128)} %bitcast.1.lent_flag, bf16[4,552,128]{2,1,0:T(8,128)(2,1)S(1)} %collective-permute-done.refs_0_.refs_6_, bf16[4,552,128]{2,1,0:T(8,128)(2,1)S(1)} %collective-permute-done.1.refs_1_.refs_7_, ...), custom_call_target="tpu_custom_call" | custom-call | flops 1000 | bytes 1000 | tf_op jit(solution)/shard_map/lon_rows/pallas_call | solution.py:196
  65.8 0.7 collective-permute-start.12
  66.5 0.7 collective-permute-start.6
  67.2 15.9 %collective-permute-done.9.refs_1_ = bf16[4,552,128]{2,1,0:T(8,128)(2,1)S(1)} collective-permute-done((bf16[4,552,128]{2,1,0:T(8,128)(2,1)S(1)}, bf16[4,552,128]{2,1,0:T(8,128)(2,1)S(1)}, u32[]{:S(2)}, u32[]{:S(2)}) %collective-permute-start.9) | collective-permute-done | bytes 565280 | tf_op jit(solution)/shard_map/ppermute | solution.py:41
  83.1 1.6 %lon_rows.3.mid = bf16[4,552,256]{2,1,0:T(8,128)(2,1)S(1)} custom-call(s32[1]{0:T(128)} %bitcast.1.lent_flag, bf16[4,552,128]{2,1,0:T(8,128)(2,1)S(1)} %collective-permute-done.8.refs_0_, bf16[4,552,128]{2,1,0:T(8,128)(2,1)S(1)} %collective-permute-done.9.refs_1_, bf16[4,552,128]{2,1,0:T(8,128)(2,1)S(1)} %collective-permute-done.10.refs_2_, ...), custom_call_target="tpu_custom_call" | custom-call | flops 1000 | bytes 1000 | tf_op jit(solution)/shard_map/lon_rows/pallas_call | solution.py:196
  84.7 0.0 copy-start.1
  84.7 2.8 %lat_rows.1 = bf16[548,8,256]{2,1,0:T(8,128)(2,1)S(1)} custom-call(bf16[2,552,256]{2,1,0:T(8,128)(2,1)S(1)} %collective-permute-done.6.above, bf16[2,552,256]{2,1,0:T(8,128)(2,1)S(1)} %get-tuple-element.21.refs_6_.top, bf16[4,552,256]{2,1,0:T(8,128)(2,1)S(1)} %lon_rows.3.mid, bf16[2,552,256]{2,1,0:T(8,128)(2,1)S(1)} %get-tuple-element.20.bot, ...), custom_call_target="tpu_custom_call" | custom-call | flops 1000 | bytes 1000 | tf_op jit(solution)/shard_map/lat_rows/pallas_call | solution.py:237
  87.5 1.3 %collective-permute-start.13 = (bf16[548,8,256]{2,1,0:T(8,128)(2,1)S(1)}, bf16[548,8,256]{2,1,0:T(8,128)(2,1)S(1)}, u32[]{:S(2)}, u32[]{:S(2)}) collective-permute-start(bf16[548,8,256]{2,1,0:T(8,128)(2,1)S(1)} %lat_rows.1), channel_id=1, source_target_pairs={{0,128},{1,129},{2,130},{3,131},{4,132},{5,133},{6,134},{7,135},{8... | collective-permute-start | bytes 6733832 | tf_op jit(solution)/shard_map/ppermute | solution.py:41
  88.8 11.2 %collective-permute-done.13 = bf16[548,8,256]{2,1,0:T(8,128)(2,1)S(1)} collective-permute-done((bf16[548,8,256]{2,1,0:T(8,128)(2,1)S(1)}, bf16[548,8,256]{2,1,0:T(8,128)(2,1)S(1)}, u32[]{:S(2)}, u32[]{:S(2)}) %collective-permute-start.13) | collective-permute-done | bytes 2244640 | tf_op jit(solution)/shard_map/ppermute | solution.py:41
  100.0 2.1 %subtract_convert_fusion = bf16[548,8,256]{2,1,0:T(8,128)(2,1)} fusion(bf16[548,8,256]{2,1,0:T(8,128)(2,1)S(1)} %collective-permute-done.13, bf16[1,4,137,8,256]{4,3,2,1,0:T(8,128)(2,1)S(1)} %copy-done.1), kind=kLoop, calls=%fused_computation | loop fusion | flops 4489216 | bytes 6733824 | tf_op jit(solution)/shard_map/convert_element_type | solution.py:308
  (30 shorter events, 0.1 us)
Async XLA Ops:
  0.0 1.6 %copy-start = (bf16[1,4,137,8,256]{4,3,2,1,0:T(8,128)(2,1)S(1)}, bf16[1,4,137,8,256]{4,3,2,1,0:T(8,128)(2,1)}, u32[]{:S(2)}) copy-start(bf16[1,4,137,8,256]{4,3,2,1,0:T(8,128)(2,1)} %param.8) | copy-start | bytes 6733828
  1.6 13.2 %copy-start.8 = (s32[1,8,256]{2,1,0:T(8,128)S(1)}, s32[1,8,256]{2,1,0:T(8,128)}, u32[]{:S(2)}) copy-start(s32[1,8,256]{2,1,0:T(8,128)} %param.14) | copy-start | bytes 24580
  1.6 13.2 %copy-start.9 = (s32[1,8,2,6]{1,2,3,0:T(2,128)S(1)}, s32[1,8,2,6]{1,2,3,0:T(2,128)}, u32[]{:S(2)}) copy-start(s32[1,8,2,6]{1,2,3,0:T(2,128)} %param.10) | copy-start | bytes 1156
  1.6 21.0 %copy-start.6 = (s32[1,8,256]{2,1,0:T(8,128)S(1)}, s32[1,8,256]{2,1,0:T(8,128)}, u32[]{:S(2)}) copy-start(s32[1,8,256]{2,1,0:T(8,128)} %param.12) | copy-start | bytes 24580
  1.6 21.0 %copy-start.7 = (s32[1,8,256]{2,1,0:T(8,128)S(1)}, s32[1,8,256]{2,1,0:T(8,128)}, u32[]{:S(2)}) copy-start(s32[1,8,256]{2,1,0:T(8,128)} %param.11) | copy-start | bytes 24580
  1.6 21.2 %copy-start.4 = (f32[1,8,256]{2,1,0:T(8,128)S(1)}, f32[1,8,256]{2,1,0:T(8,128)}, u32[]{:S(2)}) copy-start(f32[1,8,256]{2,1,0:T(8,128)} %param.15) | copy-start | bytes 24580
  1.7 21.2 %copy-start.5 = (f32[1,8,256]{2,1,0:T(8,128)S(1)}, f32[1,8,256]{2,1,0:T(8,128)}, u32[]{:S(2)}) copy-start(f32[1,8,256]{2,1,0:T(8,128)} %param.13) | copy-start | bytes 24580
  4.0 0.8 copy-start.2
  4.8 14.9 %collective-permute-start.2 = (bf16[4,552,256]{2,1,0:T(8,128)(2,1)S(1)}, bf16[4,552,256]{2,1,0:T(8,128)(2,1)S(1)}, u32[]{:S(2)}, u32[]{:S(2)}) collective-permute-start(bf16[4,552,256]{2,1,0:T(8,128)(2,1)S(1)} %get-tuple-element.17.own_ref), channel_id=1, source_target_pairs={{128,384},{129,385},{130,386},{131,387},{132,388},{133,389},{134,3... | collective-permute-start | bytes 3391496 | tf_op jit(solution)/shard_map/ppermute | solution.py:41
  7.2 34.1 %collective-permute-start.7 = (bf16[4,552,256]{2,1,0:T(8,128)(2,1)}, bf16[4,552,256]{2,1,0:T(8,128)(2,1)}, u32[]{:S(2)}, u32[]{:S(2)}) collective-permute-start(bf16[4,552,256]{2,1,0:T(8,128)(2,1)} %get-tuple-element.22.own_ref), channel_id=1, source_target_pairs={{128,384},{129,385},{130,386},{131,387},{132,388},{133,389},{134,3... | collective-permute-start | bytes 3391496 | tf_op jit(solution)/shard_map/ppermute | solution.py:41
  9.5 36.1 %collective-permute-start = (bf16[4,552,128]{2,1,0:T(8,128)(2,1)S(1)}, bf16[4,552,128]{2,1,0:T(8,128)(2,1)S(1)}, u32[]{:S(2)}, u32[]{:S(2)}) collective-permute-start(bf16[4,552,128]{2,1,0:T(8,128)(2,1)S(1)} %get-tuple-element.16.own_east_ref), channel_id=1, source_target_pairs={{0,2},{1,3},{2,4},{3,5},{4,6},{5,7},{6,8},{7,9},{8,10},{9,11},{10,... | collective-permute-start | bytes 1695752 | tf_op jit(solution)/shard_map/ppermute | solution.py:41
  14.9 26.5 %copy-start.3 = (bf16[4,552,128]{2,1,0:T(8,128)(2,1)S(1)}, bf16[4,552,128]{2,1,0:T(8,128)(2,1)}, u32[]{:S(2)}) copy-start(bf16[4,552,128]{2,1,0:T(8,128)(2,1)} %copy-done.2) | copy-start | bytes 1695748
  21.2 43.2 %collective-permute-start.4 = (bf16[4,552,256]{2,1,0:T(8,128)(2,1)S(1)}, bf16[4,552,256]{2,1,0:T(8,128)(2,1)S(1)}, u32[]{:S(2)}, u32[]{:S(2)}) collective-permute-start(bf16[4,552,256]{2,1,0:T(8,128)(2,1)S(1)} %get-tuple-element.19.refs_4_.refs_10_), channel_id=1, source_target_pairs={{0,1},{1,2},{2,3},{3,4},{4,5},{5,6},{6,7},{7,8},{8,9},{9,10},{10,1... | collective-permute-start | bytes 3391496 | tf_op jit(solution)/shard_map/ppermute | solution.py:41
  22.0 19.4 %collective-permute-start.3 = (bf16[4,552,128]{2,1,0:T(8,128)(2,1)S(1)}, bf16[4,552,128]{2,1,0:T(8,128)(2,1)S(1)}, u32[]{:S(2)}, u32[]{:S(2)}) collective-permute-start(bf16[4,552,128]{2,1,0:T(8,128)(2,1)S(1)} %get-tuple-element.18), channel_id=1, source_target_pairs={{0,31},{1,0},{2,1},{3,2},{4,3},{5,4},{6,5},{7,6},{8,7},{9,8},{10,9... | collective-permute-start | bytes 1695752 | tf_op jit(solution)/shard_map/ppermute | solution.py:41
  22.9 18.5 %collective-permute-start.5 = (f32[4,8,256]{2,1,0:T(8,128)S(1)}, f32[4,8,256]{2,1,0:T(8,128)S(1)}, u32[]{:S(2)}, u32[]{:S(2)}) collective-permute-start(f32[4,8,256]{2,1,0:T(8,128)S(1)} %pad_maximum_fusion), channel_id=1, source_target_pairs={{128,384},{129,385},{130,386},{131,387},{132,388},{133,389},{134,3... | collective-permute-start | bytes 98312 | tf_op jit(solution)/shard_map/ppermute | solution.py:41
  43.7 19.4 %collective-permute-start.8 = (bf16[4,552,128]{2,1,0:T(8,128)(2,1)S(1)}, bf16[4,552,128]{2,1,0:T(8,128)(2,1)S(1)}, u32[]{:S(2)}, u32[]{:S(2)}) collective-permute-start(bf16[4,552,128]{2,1,0:T(8,128)(2,1)S(1)} %get-tuple-element.24), channel_id=1, source_target_pairs={{0,2},{1,3},{2,4},{3,5},{4,6},{5,7},{6,8},{7,9},{8,10},{9,11},{10,... | collective-permute-start | bytes 1695752 | tf_op jit(solution)/shard_map/ppermute | solution.py:41
  45.6 18.8 %collective-permute-start.1 = (bf16[4,552,128]{2,1,0:T(8,128)(2,1)S(1)}, bf16[4,552,128]{2,1,0:T(8,128)(2,1)S(1)}, u32[]{:S(2)}, u32[]{:S(2)}) collective-permute-start(bf16[4,552,128]{2,1,0:T(8,128)(2,1)S(1)} %collective-permute-done.refs_0_.refs_6_), channel_id=1, source_target_pairs={{128,384},{129,385},{130,386},{131,387},{132,388},{133,389},{134,3... | collective-permute-start | bytes 1695752 | tf_op jit(solution)/shard_map/ppermute | solution.py:41
  49.7 33.4 %collective-permute-start.11 = (bf16[4,552,256]{2,1,0:T(8,128)(2,1)S(1)}, bf16[4,552,256]{2,1,0:T(8,128)(2,1)S(1)}, u32[]{:S(2)}, u32[]{:S(2)}) collective-permute-start(bf16[4,552,256]{2,1,0:T(8,128)(2,1)S(1)} %get-tuple-element.26.refs_4_), channel_id=1, source_target_pairs={{0,1},{1,2},{2,3},{3,4},{4,5},{5,6},{6,7},{7,8},{8,9},{9,10},{10,1... | collective-permute-start | bytes 3391496 | tf_op jit(solution)/shard_map/ppermute | solution.py:41
  52.6 14.6 %collective-permute-start.10 = (bf16[4,552,128]{2,1,0:T(8,128)(2,1)S(1)}, bf16[4,552,128]{2,1,0:T(8,128)(2,1)S(1)}, u32[]{:S(2)}, u32[]{:S(2)}) collective-permute-start(bf16[4,552,128]{2,1,0:T(8,128)(2,1)S(1)} %get-tuple-element.25), channel_id=1, source_target_pairs={{0,31},{1,0},{2,1},{3,2},{4,3},{5,4},{6,5},{7,6},{8,7},{9,8},{10,9... | collective-permute-start | bytes 1695752 | tf_op jit(solution)/shard_map/ppermute | solution.py:41
  63.1 19.9 %collective-permute-start.9 = (bf16[4,552,128]{2,1,0:T(8,128)(2,1)S(1)}, bf16[4,552,128]{2,1,0:T(8,128)(2,1)S(1)}, u32[]{:S(2)}, u32[]{:S(2)}) collective-permute-start(bf16[4,552,128]{2,1,0:T(8,128)(2,1)S(1)} %collective-permute-done.8.refs_0_), channel_id=1, source_target_pairs={{128,384},{129,385},{130,386},{131,387},{132,388},{133,389},{134,3... | collective-permute-start | bytes 1695752 | tf_op jit(solution)/shard_map/ppermute | solution.py:41
  65.8 18.9 %collective-permute-start.12 = (bf16[2,552,256]{2,1,0:T(8,128)(2,1)S(1)}, bf16[2,552,256]{2,1,0:T(8,128)(2,1)S(1)}, u32[]{:S(2)}, u32[]{:S(2)}) collective-permute-start(bf16[2,552,256]{2,1,0:T(8,128)(2,1)S(1)} %get-tuple-element.21.refs_6_.top), channel_id=1, source_target_pairs={{32,0},{33,1},{34,2},{35,3},{36,4},{37,5},{38,6},{39,7},{40,8},{41... | collective-permute-start | bytes 1695752 | tf_op jit(solution)/shard_map/ppermute | solution.py:41
  66.5 18.3 %collective-permute-start.6 = (bf16[2,552,256]{2,1,0:T(8,128)(2,1)S(1)}, bf16[2,552,256]{2,1,0:T(8,128)(2,1)S(1)}, u32[]{:S(2)}, u32[]{:S(2)}) collective-permute-start(bf16[2,552,256]{2,1,0:T(8,128)(2,1)S(1)} %get-tuple-element.20.bot), channel_id=1, source_target_pairs={{0,32},{1,33},{2,34},{3,35},{4,36},{5,37},{6,38},{7,39},{8,40},{9,... | collective-permute-start | bytes 1695752 | tf_op jit(solution)/shard_map/ppermute | solution.py:41
  84.7 15.3 %copy-start.1 = (bf16[1,4,137,8,256]{4,3,2,1,0:T(8,128)(2,1)S(1)}, bf16[1,4,137,8,256]{4,3,2,1,0:T(8,128)(2,1)}, u32[]{:S(2)}) copy-start(bf16[1,4,137,8,256]{4,3,2,1,0:T(8,128)(2,1)} %param.8) | copy-start | bytes 6733828
  87.5 12.5 %collective-permute-start.13 = (bf16[548,8,256]{2,1,0:T(8,128)(2,1)S(1)}, bf16[548,8,256]{2,1,0:T(8,128)(2,1)S(1)}, u32[]{:S(2)}, u32[]{:S(2)}) collective-permute-start(bf16[548,8,256]{2,1,0:T(8,128)(2,1)S(1)} %lat_rows.1), channel_id=1, source_target_pairs={{0,128},{1,129},{2,130},{3,131},{4,132},{5,133},{6,134},{7,135},{8... | collective-permute-start | bytes 6733832 | tf_op jit(solution)/shard_map/ppermute | solution.py:41
